TPU v7x, 32 devices: a whole 2x2x4 slice. The times are simulated.
32 devices in a mesh: dp: 8 (over z, y), expert: 2 (over core), tensor: 2 (over x).
Axes of the slice: x: 2, y: 2, z: 4, core: 2. Of those that a mesh axis runs over, the one named last changes fastest.
Arguments:
- tokens: bfloat16 [16384, 768], P(('dp', 'expert'), 'tensor'), may hold values from -6 to 6
- gain_attn: float32 [768], replicated, may hold values from 0.5 to 1.5
- w_query: bfloat16 [768, 768], P(None, 'tensor'), may hold values from -0.21875 to 0.21875
- w_key: bfloat16 [768, 768], P(None, 'tensor'), may hold values from -0.21875 to 0.21875
- w_value: bfloat16 [768, 768], P(None, 'tensor'), may hold values from -0.21875 to 0.21875
- w_output: bfloat16 [768, 768], P('tensor'), may hold values from -1.75 to 1.75
- gain_moe: float32 [768], replicated, may hold values from 0.5 to 1.5
- w_router: bfloat16 [768, 8], replicated, may hold values from -0.14941406 to 0.14941406
- w_in: bfloat16 [8, 768, 3072], P('expert', None, 'tensor'), may hold values from -0.21875 to 0.21875
- w_out: bfloat16 [8, 3072, 768], P('expert', 'tensor'), may hold values from -0.109375 to 0.109375
- routes: int32 [16384, 2], P(('dp', 'expert')), may hold values from 0 to 7, all different within a row; in each aligned block of 1024 rows (0 to 1023, 1024 to 2047, ...) at most 320 rows name the same one
- cotangent: bfloat16 [16384, 768], P(('dp', 'expert'), 'tensor'), may hold values from -6 to 6
Outputs:
- mixed: bfloat16 [16384, 768], P(('dp', 'expert'), 'tensor')
- grad_tokens: float32 [16384, 768], P(('dp', 'expert'), 'tensor')
- grad_gain_attn: float32 [768], P('tensor')
- grad_query: float32 [768, 768], P(None, 'tensor')
- grad_key: float32 [768, 768], P(None, 'tensor')
- grad_value: float32 [768, 768], P(None, 'tensor')
- grad_output: float32 [768, 768], P('tensor')
- grad_gain_moe: float32 [768], replicated
- grad_router: float32 [768, 8], replicated
- grad_in: float32 [8, 768, 3072], P('expert', 'dp', 'tensor')
- grad_out: float32 [8, 3072, 768], P('expert', 'tensor', 'dp')
Inputs may be any that keep to these rules, and one draw needn't show every extreme that they name: `routes`: each row names 2 different experts. In each aligned block of 1024 rows (one sequence) no expert is named by more than 320 rows, a bound that some block reaches.
All inputs are finite; a program needn't handle non-finite values.
Results may differ from a plain program's by a relative error of at most 0.015.
Values may be sent and summed in bfloat16 or wider, within the bound.
A program may use at most 256 MiB of HBM per device.

v0:
```python
import math

import jax
import jax.numpy as jnp
from jax import lax
from jax.sharding import PartitionSpec as P

D = 768
DH = 64
TOP = 2


epsilon = 1e-06
highest = lax.Precision.HIGHEST


def rms_scale(rows):
    return lax.rsqrt(jnp.mean(rows * rows, axis=-1, keepdims=True) + epsilon)


def slot_index(routes, experts, capacity):
    flat = routes.reshape(-1)
    onehot = (flat[:, None] == jnp.arange(experts, dtype=jnp.int32)[None, :]).astype(jnp.int32)
    before = jnp.cumsum(onehot, axis=0) - onehot
    position = jnp.sum(before * onehot, axis=1)
    return flat * capacity + position


def local(
    tokens,
    gain_attn,
    w_query,
    w_key,
    w_value,
    w_output,
    gain_moe,
    w_router,
    w_in,
    w_out,
    routes,
    cotangent,
):
    bf16 = jnp.bfloat16
    f32 = jnp.float32
    width = tokens.shape[1]
    column = lax.axis_index("tensor") * width
    whole_in, whole_cot = (
        lax.all_gather(tokens, "tensor", axis=1, tiled=True),
        lax.all_gather(cotangent, "tensor", axis=1, tiled=True),
    )
    residual = whole_in.astype(f32)
    grad_top = whole_cot.astype(f32)
    seq_len = residual.shape[0]
    scale_one = rms_scale(residual)
    normed_one = residual * scale_one
    low_one = (normed_one * gain_attn).astype(bf16)
    heads_dev = w_query.shape[1] // DH
    query = (
        jnp.dot(low_one, w_query, preferred_element_type=f32)
        .astype(bf16)
        .reshape(seq_len, heads_dev, DH)
    )
    key_rows = (
        jnp.dot(low_one, w_key, preferred_element_type=f32)
        .astype(bf16)
        .reshape(seq_len, heads_dev, DH)
    )
    value_rows = (
        jnp.dot(low_one, w_value, preferred_element_type=f32)
        .astype(bf16)
        .reshape(seq_len, heads_dev, DH)
    )
    block = min(512, seq_len)
    nblocks = seq_len // block
    factor = 1.0 / math.sqrt(DH)

    def block_scores(start):
        query_block = lax.dynamic_slice_in_dim(query, start, block, 0)
        scores = (
            jnp.einsum("qhd,khd->hqk", query_block, key_rows, preferred_element_type=f32) * factor
        )
        rows_at = start + jnp.arange(block, dtype=jnp.int32)[:, None]
        cols_at = jnp.arange(seq_len, dtype=jnp.int32)[None, :]
        return (jnp.where(cols_at <= rows_at, scores, -1e30), query_block)

    def attend(index):
        scores, _ = block_scores(index * block)
        peak = jnp.max(scores, axis=-1, keepdims=True)
        expo = jnp.exp(scores - peak)
        total = jnp.sum(expo, axis=-1, keepdims=True)
        prob = (expo / total).astype(bf16)
        result = jnp.einsum("hqk,khd->qhd", prob, value_rows, preferred_element_type=f32)
        return (result.astype(bf16), (peak + jnp.log(total))[..., 0])

    block_out, log_total = lax.map(attend, jnp.arange(nblocks, dtype=jnp.int32))
    heads_out = block_out.reshape(seq_len, heads_dev * DH)
    attn_part = jnp.dot(heads_out, w_output, preferred_element_type=f32)
    hidden = residual + lax.psum(attn_part, "tensor")
    scale_two = rms_scale(hidden)
    normed_two = hidden * scale_two
    low_two = (normed_two * gain_moe).astype(bf16)
    logits = jnp.dot(low_two, w_router, preferred_element_type=f32)
    experts = w_router.shape[1]
    capacity = 5 * TOP * seq_len // (4 * experts)
    picks = (routes[:, :, None] == jnp.arange(experts, dtype=jnp.int32)[None, None, :]).astype(f32)
    chosen = jnp.einsum("ske,se->sk", picks, logits, precision=highest)
    peak_gate = jnp.max(chosen, axis=1, keepdims=True)
    expo_gate = jnp.exp(chosen - peak_gate)
    gates = expo_gate / jnp.sum(expo_gate, axis=1, keepdims=True)
    place = slot_index(routes, experts, capacity)
    doubled = jnp.repeat(low_two, TOP, axis=0)
    send = (
        jnp.zeros((experts * capacity, D), bf16)
        .at[place]
        .set(doubled)
        .reshape(experts, capacity, D)
    )
    arrived = lax.all_to_all(send, "expert", split_axis=0, concat_axis=1, tiled=True)
    pre = jnp.einsum("erd,edf->erf", arrived, w_in, preferred_element_type=f32)
    active = jax.nn.gelu(pre).astype(bf16)
    out_part = jnp.einsum("erf,efd->erd", active, w_out, preferred_element_type=f32)
    returned = lax.all_to_all(
        out_part.astype(jnp.bfloat16), "expert", split_axis=1, concat_axis=0, tiled=True
    ).astype(out_part.dtype)
    kept = returned.reshape(experts * capacity, D)[place].reshape(seq_len, TOP, D)
    gated_part = jnp.sum(gates[:, :, None] * kept, axis=1)
    moe_cols = lax.psum_scatter(
        gated_part.astype(jnp.bfloat16), "tensor", scatter_dimension=1, tiled=True
    ).astype(jnp.float32)
    hidden_cols = lax.dynamic_slice_in_dim(hidden, column, width, 1)
    mixed = (hidden_cols + moe_cols).astype(bf16)
    gate_grad_part = jnp.sum(kept * grad_top[:, None, :], axis=2)
    slot_grad = (gates[:, :, None] * grad_top[:, None, :]).astype(bf16).reshape(seq_len * TOP, D)
    grad_send = (
        jnp.zeros((experts * capacity, D), bf16)
        .at[place]
        .set(slot_grad)
        .reshape(experts, capacity, D)
    )
    grad_arrived = lax.all_to_all(grad_send, "expert", split_axis=0, concat_axis=1, tiled=True)
    grad_active = jnp.einsum("erd,efd->erf", grad_arrived, w_out, preferred_element_type=f32)
    grad_w_out = jnp.einsum("erf,erd->efd", active, grad_arrived, preferred_element_type=f32)
    _, pull_gelu = jax.vjp(jax.nn.gelu, pre)
    grad_pre = pull_gelu(grad_active)[0].astype(bf16)
    grad_w_in = jnp.einsum("erd,erf->edf", arrived, grad_pre, preferred_element_type=f32)
    grad_arrived_part = jnp.einsum("erf,edf->erd", grad_pre, w_in, preferred_element_type=f32)
    grad_returned = lax.all_to_all(
        grad_arrived_part, "expert", split_axis=1, concat_axis=0, tiled=True
    )
    grad_two_part = jnp.sum(
        grad_returned.reshape(experts * capacity, D)[place].reshape(seq_len, TOP, D), axis=1
    )
    grad_two_sum, gate_grad = lax.psum((grad_two_part, gate_grad_part), "tensor")
    gate_mean = jnp.sum(gates * gate_grad, axis=1, keepdims=True)
    grad_chosen = gates * (gate_grad - gate_mean)
    grad_logits = jnp.einsum("ske,sk->se", picks, grad_chosen, precision=highest)
    router_wide = w_router.astype(f32)
    grad_two = grad_two_sum + jnp.dot(grad_logits, router_wide.T, precision=highest)
    grad_router = jnp.dot(low_two.astype(f32).T, grad_logits, precision=highest)
    grad_gain_moe = jnp.sum(grad_two * normed_two, axis=0)
    scaled_two = grad_two * gain_moe
    grad_hidden = grad_top + scale_two * (
        scaled_two - normed_two * jnp.mean(normed_two * scaled_two, axis=1, keepdims=True)
    )
    grad_attn = grad_hidden.astype(bf16)
    grad_heads = jnp.dot(grad_attn, w_output.T, preferred_element_type=f32).astype(bf16)
    grad_w_output = jnp.dot(heads_out.T, grad_attn, preferred_element_type=f32)
    grad_heads = grad_heads.reshape(seq_len, heads_dev, DH)

    def attend_back(carry, index):
        grad_key_sum, grad_value_sum = carry
        start = index * block
        scores, query_block = block_scores(start)
        log_block = lax.dynamic_index_in_dim(log_total, index, 0, keepdims=False)
        prob = jnp.exp(scores - log_block[..., None])
        grad_block = lax.dynamic_slice_in_dim(grad_heads, start, block, 0)
        grad_prob = jnp.einsum("qhd,khd->hqk", grad_block, value_rows, preferred_element_type=f32)
        grad_score = (
            prob * (grad_prob - jnp.sum(prob * grad_prob, axis=-1, keepdims=True))
        ).astype(bf16)
        grad_query_block = (
            jnp.einsum("hqk,khd->qhd", grad_score, key_rows, preferred_element_type=f32) * factor
        ).astype(bf16)
        grad_key_sum = (
            grad_key_sum
            + jnp.einsum("hqk,qhd->khd", grad_score, query_block, preferred_element_type=f32)
            * factor
        )
        grad_value_sum = grad_value_sum + jnp.einsum(
            "hqk,qhd->khd", prob.astype(bf16), grad_block, preferred_element_type=f32
        )
        return ((grad_key_sum, grad_value_sum), grad_query_block)

    zeros = jnp.zeros((seq_len, heads_dev, DH), f32)
    (grad_key_rows, grad_value_rows), grad_query_blocks = lax.scan(
        attend_back, (zeros, zeros), jnp.arange(nblocks, dtype=jnp.int32)
    )
    grad_query_rows = grad_query_blocks.reshape(seq_len, heads_dev * DH)
    grad_key_rows = grad_key_rows.reshape(seq_len, heads_dev * DH).astype(bf16)
    grad_value_rows = grad_value_rows.reshape(seq_len, heads_dev * DH).astype(bf16)
    grad_w_query = jnp.dot(low_one.T, grad_query_rows, preferred_element_type=f32)
    grad_w_key = jnp.dot(low_one.T, grad_key_rows, preferred_element_type=f32)
    grad_w_value = jnp.dot(low_one.T, grad_value_rows, preferred_element_type=f32)
    grad_one = jnp.dot(grad_query_rows, w_query.T, preferred_element_type=f32)
    grad_one = grad_one + jnp.dot(grad_key_rows, w_key.T, preferred_element_type=f32)
    grad_one = grad_one + jnp.dot(grad_value_rows, w_value.T, preferred_element_type=f32)
    gain_part = jnp.sum(grad_one * normed_one, axis=0)
    scaled_one = grad_one * gain_attn
    grad_in_part = scale_one * (
        scaled_one - normed_one * jnp.mean(normed_one * scaled_one, axis=1, keepdims=True)
    )
    grad_in_cols, gain_share = (
        lax.psum_scatter(
            grad_in_part.astype(jnp.bfloat16), "tensor", scatter_dimension=1, tiled=True
        ).astype(jnp.float32),
        lax.psum_scatter(
            gain_part[None, :].astype(jnp.bfloat16), "tensor", scatter_dimension=1, tiled=True
        ).astype(jnp.float32),
    )
    grad_tokens = lax.dynamic_slice_in_dim(grad_hidden, column, width, 1) + grad_in_cols
    summed_dense = lax.psum(
        (
            grad_w_query,
            grad_w_key,
            grad_w_value,
            grad_w_output,
            gain_share[0],
            grad_gain_moe,
            grad_router,
        ),
        ("dp", "expert"),
    )
    grad_in_share, grad_out_share = (
        lax.psum_scatter(
            grad_w_in.astype(jnp.bfloat16), "dp", scatter_dimension=1, tiled=True
        ).astype(jnp.float32),
        lax.psum_scatter(
            grad_w_out.astype(jnp.bfloat16), "dp", scatter_dimension=2, tiled=True
        ).astype(jnp.float32),
    )
    return (
        mixed,
        grad_tokens,
        summed_dense[4],
        summed_dense[0],
        summed_dense[1],
        summed_dense[2],
        summed_dense[3],
        summed_dense[5],
        summed_dense[6],
        grad_in_share,
        grad_out_share,
    )


def solution(mesh):
    in_specs = (
        P(("dp", "expert"), "tensor"),
        P(),
        P(None, "tensor"),
        P(None, "tensor"),
        P(None, "tensor"),
        P("tensor", None),
        P(),
        P(),
        P("expert", None, "tensor"),
        P("expert", "tensor", None),
        P(("dp", "expert"), None),
        P(("dp", "expert"), "tensor"),
    )
    out_specs = (
        P(("dp", "expert"), "tensor"),
        P(("dp", "expert"), "tensor"),
        P("tensor"),
        P(None, "tensor"),
        P(None, "tensor"),
        P(None, "tensor"),
        P("tensor", None),
        P(),
        P(),
        P("expert", "dp", "tensor"),
        P("expert", "tensor", "dp"),
    )
    return jax.shard_map(local, mesh=mesh, in_specs=in_specs, out_specs=out_specs, check_vma=False)
```

profile of v0, /device:TPU:0, one launch (start us, length us, event | category | flops | bytes accessed | tf_op | source)
XLA Modules:
  0.0 1048.3 jit_solution(16143599807944752334)
XLA Ops:
  8.8 30.8 %all-gather.3.cloned.1.call-done = bf16[1024,768]{1,0:T(8,128)(2,1)} async-done(((bf16[1024,384]{1,0:T(8,128)(2,1)}), bf16[1024,768]{1,0:T(8,128)(2,1)}) %all-gather.3.cloned.1.call-update) | async-done | bytes 1572880 | tf_op jit(solution)/shard_map/all_gather | solution.py:48
  46.9 26.0 %while.27 = (s32[]{:T(128)}, bf16[2,512,6,64]{1,3,2,0:T(8,128)(2,1)}, f32[2,6,512]{2,1,0:T(8,128)S(1)}, s32[2]{0:T(128)S(1)}, bf16[1024,6,64]{0,2,1:T(8,128)(2,1...) while((s32[]{:T(128)}, ...), condition=%wide.region_4.5_spmd, body=%wide.region_1.4_spmd.sunk | while | flops 843773440 | bytes 48619768 | solution.py:95
  50.9 3.6 fusion.144
  54.6 4.4 fusion.145
  63.9 3.6 fusion.144
  67.6 4.4 fusion.145
  72.9 2.6 copy.40
  76.6 2.7 fusion.77
  80.7 2.5 reduce-window.6
  83.9 6.2 mul.255
  90.1 8.5 mul.256
  98.7 3.4 convert_element_type.155
  102.0 63.2 %all-reduce.6.cloned.1.call-done = f32[1024,768]{1,0:T(8,128)} async-done(((f32[1024,768]{1,0:T(8,128)}), f32[1024,768]{1,0:T(8,128)}) %all-reduce.6.cloned.1.call-update) | async-done | bytes 3145744 | tf_op jit(solution)/shard_map/psum | solution.py:98
  169.3 5.8 fusion.56
  176.9 3.3 broadcast_in_dim.34
  180.2 7.6 reshape.243
  187.8 25.0 %scatter_custom_fusion = bf16[2560,768]{1,0:T(8,128)(2,1)} fusion(s32[2048]{0:T(1024)S(1)} %bitcast.209, bf16[2048,768]{1,0:T(8,128)(2,1)} %reshape.243, bf16[]{:T(256)} %constant.54.clone.1), kind=kCustom, calls=%fused_computation.87 | custom fusion | bytes 3932672 | tf_op jit(solution)/shard_map/scatter | solution.py:115
  212.8 8.2 all_to_all.60
  223.2 13.7 %scatter_custom_fusion.1 = bf16[2560,768]{1,0:T(8,128)(2,1)} fusion(s32[2048]{0:T(1024)S(1)} %bitcast.210, f32[2048,768]{1,0:T(8,128)} %mul.256, f32[2048]{0:T(1024)S(1)} %mul.253, bf16[]{:T(256)} %constant.54.clone.1), kind=kCustom, calls=%fused_computation.77 | custom fusion | flops 3145728 | bytes 10231810 | tf_op jit(solution)/shard_map/scatter | solution.py:137
  236.9 8.2 all_to_all.61
  245.5 14.7 %fusion.79 = f32[4,640,1536]{2,1,0:T(8,128)} fusion(bf16[4,640,768]{2,1,0:T(8,128)(2,1)S(1)} %bitcast.190, bf16[4,1536,768]{2,1,0:T(8,128)(2,1)} %param.25), kind=kOutput, calls=%fused_computation.132 | convolution fusion | flops 6039797760 | bytes 29097984 | tf_op jit(solution)/shard_map/erd,efd->erf/dot_general | solution.py:141
  260.2 24.3 %fusion.38 = (bf16[4,640,1536]{2,1,0:T(8,128)(2,1)}, f32[4,640,1536]{2,1,0:T(8,128)}) fusion(f32[4,640,1536]{2,1,0:T(8,128)} %fusion.79, bf16[4,640,768]{2,1,0:T(8,128)(2,1)} %bitcast.188, bf16[4,768,1536]{2,1,0:T(8,128)(2,1)} %param.24), kind=kOutput, calls=%fused_computation.56 | convolution fusion | flops 6118440960 | bytes 52690944 | tf_op jit(solution)/shard_map/erd,edf->erf/dot_general | solution.py:119
  284.4 13.6 %fusion.80 = f32[4,640,768]{2,1,0:T(8,128)} fusion(bf16[4,640,1536]{2,1,0:T(8,128)(2,1)} %get-tuple-element.194, bf16[4,768,1536]{2,1,0:T(8,128)(2,1)} %param.24), kind=kOutput, calls=%fused_computation.133 | convolution fusion | flops 6039797760 | bytes 25165824 | tf_op jit(solution)/shard_map/erf,edf->erd/dot_general | solution.py:146
  298.0 8.3 copy.49
  306.3 10.1 all_to_all.62
  316.4 4.6 copy.50
  321.0 13.8 %gather_fusion.1 = f32[2048,768]{1,0:T(8,128)} fusion(f32[2560,768]{1,0:T(8,128)} %bitcast.168, s32[2048]{0:T(1024)S(1)} %broadcast_clamp_fusion), kind=kCustom, calls=%fused_computation.1 | custom fusion | bytes 12591104 | tf_op jit(solution)/shard_map/gather | solution.py:151
  334.9 8.1 reshape.217
  343.0 11.9 %reduce_sum.134 = f32[1024,768]{1,0:T(8,128)} reduce(f32[1024,2,768]{2,1,0:T(2,128)} %reshape.217, f32[]{:T(128)} %constant.55.clone.1), dimensions={1}, to_apply=%region_16.17 | reduce | flops 786432 | bytes 9437188 | tf_op jit(solution)/shard_map/reduce_sum | solution.py:150
  355.0 14.1 %convolution_convert_fusion.2 = bf16[4,640,768]{2,1,0:T(8,128)(2,1)S(1)} fusion(bf16[4,1536,768]{2,1,0:T(8,128)(2,1)} %param.25, f32[4,640,1536]{2,1,0:T(8,128)} %get-tuple-element.195), kind=kOutput, calls=%fused_computation.85 | convolution fusion | flops 6077153280 | bytes 29097984 | tf_op jit(solution)/shard_map/erf,efd->erd/dot_general | solution.py:121
  369.0 3.0 copy.46
  372.1 7.1 all_to_all.63
  379.1 3.8 copy.47
  383.0 13.8 %gather_fusion = f32[2048,768]{1,0:T(8,128)} fusion(f32[2560,768]{1,0:T(8,128)} %bitcast.167, s32[2048]{0:T(1024)S(1)} %broadcast_clamp_fusion), kind=kCustom, calls=%fused_computation | custom fusion | bytes 12591104 | tf_op jit(solution)/shard_map/gather | solution.py:125
  396.8 8.3 reshape.214
  405.1 16.6 %multiply_reduce_fusion.1 = (f32[1024,2]{1,0:T(8,128)}, bf16[1024,768]{1,0:T(8,128)(2,1)S(1)}) fusion(f32[1024,2,768]{2,1,0:T(2,128)} %reshape.214, f32[1024,768]{1,0:T(8,128)} %convert_element_type.155, f32[1024,2]{1,0:T(8,128)S(1)} %fusion.62), kind=kLoop, calls=%fused_computation.60 | loop fusion | flops 5502976 | bytes 11026432 | tf_op jit(solution)/shard_map/reduce_sum | solution.py:132
  423.3 28.7 %psum.72 = f32[1024,2]{1,0:T(8,128)S(1)} all-reduce(f32[1024,2]{1,0:T(8,128)} %get-tuple-element.143), channel_id=1, replica_groups=mesh['dp'=8,'expert'=2,'tensor'=2] {'tensor'}, use_global_device_ids=true, to_apply=%region_19.20 | all-reduce | flops 2048 | bytes 16384 | tf_op jit(solution)/shard_map/psum | solution.py:153
  453.1 5.8 fusion.55
  459.0 5.7 multiply_reduce_fusion.3
  469.9 60.2 %while.28 = (s32[]{:T(128)}, f32[1024,6,64]{0,2,1:T(8,128)}, f32[1024,6,64]{0,2,1:T(8,128)}, bf16[2,512,6,64]{1,3,2,0:T(8,128)(2,1)}, s32[2]{0:T(128)S(1)}, /*in...) while((s32[]{:T(128)}, f32[1024,6,64]{0,2,1:T(8,128)}, ...), condition=%wide.region_24.25_spmd.clone, body=%wide.region_22.24_spmd.clone.sunk | while | flops 2063332864 | bytes 138637680 | solution.py:195
  475.8 4.6 bitcast_add_fusion.5
  480.3 5.4 multiply_reduce_fusion.8
  485.7 5.0 multiply_convert_fusion.8
  490.8 5.7 fusion.156
  504.3 5.7 bitcast_add_fusion.5
  510.0 5.4 multiply_reduce_fusion.8
  515.4 5.0 multiply_convert_fusion.8
  520.4 5.7 fusion.156
  526.1 3.8 bitcast_add_fusion.4
  536.7 3.4 fusion.48
  541.1 3.8 fusion.47
  544.9 2.6 copy.62
  547.5 15.4 %convolution_convert_fusion = bf16[4,1536,768]{1,2,0:T(8,128)(2,1)} fusion(bf16[4,640,768]{2,1,0:T(8,128)(2,1)} %bitcast.191, f32[4,640,1536]{2,1,0:T(8,128)} %get-tuple-element.195), kind=kOutput, calls=%fused_computation.58 | convolution fusion | flops 6079905792 | bytes 29097984 | tf_op jit(solution)/shard_map/erf,erd->efd/dot_general | solution.py:142
  563.0 13.5 %convolution_convert_fusion.1 = bf16[4,768,1536]{2,1,0:T(8,128)(2,1)} fusion(bf16[4,640,768]{2,1,0:T(8,128)(2,1)} %bitcast.189, bf16[4,640,1536]{2,1,0:T(8,128)(2,1)} %get-tuple-element.194), kind=kOutput, calls=%fused_computation.59 | convolution fusion | flops 6044516352 | bytes 21233664 | tf_op jit(solution)/shard_map/erd,erf->edf/dot_general | solution.py:145
  576.6 3.5 fusion.68
  590.4 2.5 add_convert_fusion
  593.9 66.1 %all-reduce = (f32[384]{0:T(512)}, f32[768]{0:T(1024)}, f32[768,8]{0,1:T(8,128)}) all-reduce(f32[384]{0:T(512)S(1)} %convert_reduce_fusion, f32[768]{0:T(1024)S(1)} %copy-done.58, f32[768,8]{0,1:T(8,128)S(1)} %fusion.83), channel_id=1, replica_groups=mesh['dp'=8,'expert'=2,'tensor'=2] {'dp','expert'}, use_global_device_ids=true, to_apply=%region_29.30 | all-reduce | flops 7296 | bytes 58368 | tf_op jit(solution)/shard_map/psum | solution.py:221
  661.5 2.7 convert_add_fusion.1
  664.2 83.9 %reduce-scatter.14.cloned.1.call-done = bf16[4,1536,96]{1,2,0:T(8,128)(2,1)} async-done(((bf16[4,1536,768]{1,2,0:T(8,128)(2,1)}), bf16[4,1536,96]{1,2,0:T(8,128)(2,1)}) %reduce-scatter.14.cloned.1.call-update) | async-done | bytes 1179664 | tf_op jit(solution)/shard_map/reduce_scatter | solution.py:237
  748.1 3.0 convert_element_type.171
  751.1 163.2 %reduce-scatter.12.cloned.1.call-done = bf16[4,96,1536]{2,1,0:T(8,128)(2,1)} async-done(((bf16[4,768,1536]{2,1,0:T(8,128)(2,1)}), bf16[4,96,1536]{2,1,0:T(8,128)(2,1)}) %reduce-scatter.12.cloned.1.call-update) | async-done | bytes 1179664 | tf_op jit(solution)/shard_map/reduce_scatter | solution.py:234
  914.3 3.0 convert_element_type.169
  917.2 118.4 %all-reduce.10.cloned.1.call-done = (f32[768,384]{1,0:T(8,128)}, f32[768,384]{1,0:T(8,128)}, f32[768,384]{1,0:T(8,128)}, f32[384,768]{1,0:T(8,128)}) async-done(((f32[768,384]{1,0:T(8,128)}, f32[768,384]{1,0:T(8,128)}, f32[768,384]{1,0:T(8,128)}, f32[384,768]{1,0:T(8,128)}), (f32[768,384]{1,0:T(8,128)}, f32[768,384]{1,0:T(8,128)}, f32[768,384]{1,0:T(8,128)}, ...) | async-done | bytes 4718608 | tf_op jit(solution)/shard_map/psum | solution.py:221
  1035.7 2.5 copy.102
  (239 shorter events, 67.7 us)
Async XLA Ops:
  7.2 34.3 %copy-start = (bf16[768,384]{1,0:T(8,128)(2,1)S(1)}, bf16[768,384]{1,0:T(8,128)(2,1)}, u32[]{:S(2)}) copy-start(bf16[768,384]{1,0:T(8,128)(2,1)} %param.20) | copy-start | bytes 1769476
  7.2 34.3 %copy-start.59 = (f32[768]{0:T(1024)S(1)}, f32[768]{0:T(1024)}, u32[]{:S(2)}) copy-start(f32[768]{0:T(1024)} %param.17) | copy-start | bytes 9220
  7.2 32.3 %all-gather.3.cloned.1.call-start = ((), (), s32[]{:S(2)}) async-start(), calls=%async_computation.9 | async-start | bytes 2359296 | tf_op jit(solution)/shard_map/all_gather | solution.py:48
  7.9 76.0 %all-gather.5.cloned.1.call-start = ((), (), s32[]{:S(2)}) async-start(), calls=%async_computation.11 | async-start | bytes 2359296 | tf_op jit(solution)/shard_map/all_gather | solution.py:49
  8.7 35.1 %copy-start.41 = (bf16[768,384]{1,0:T(8,128)(2,1)S(1)}, bf16[768,384]{1,0:T(8,128)(2,1)}, u32[]{:S(2)}) copy-start(bf16[768,384]{1,0:T(8,128)(2,1)} %param.19) | copy-start | bytes 1769476
  8.7 156.6 %all-reduce.6.cloned.1.call-start = ((), (), s32[]{:S(2)}) async-start(), calls=%async_computation.10 | async-start | bytes 6291456 | tf_op jit(solution)/shard_map/psum | solution.py:98
  39.5 4.3 copy-start.12
  41.5 3.4 copy-start.55
  50.9 3.7 copy-start.27
  63.9 3.7 copy-start.27
  72.9 6.3 copy-start.3
  72.9 6.3 copy-start.7
  72.9 6.3 copy-start.17
  72.9 6.3 copy-start.43
  72.9 3.6 copy-start.32
  76.6 2.8 copy-start.57
  79.3 379.7 %all-reduce.8.cloned.1.call-start = ((), (), s32[]{:S(2)}) async-start(), calls=%async_computation.12 | async-start | bytes 6291456 | tf_op jit(solution)/shard_map/psum | solution.py:153
  79.6 89.7 %copy-start.24 = (s32[1024,2]{1,0:T(8,128)}, s32[1024,2]{1,0:T(8,128)S(1)}, u32[]{:S(2)}) copy-start(s32[1024,2]{1,0:T(8,128)S(1)} %copy.41) | copy-start | bytes 24580
  98.7 66.6 %copy-start.13 = (bf16[1024,768]{1,0:T(8,128)(2,1)S(1)}, bf16[1024,768]{1,0:T(8,128)(2,1)}, u32[]{:S(2)}) copy-start(bf16[1024,768]{1,0:T(8,128)(2,1)} %all-gather.3.cloned.1.call-done) | copy-start | bytes 4718596
  102.0 65.7 %copy-start.53 = (f32[768]{0:T(1024)S(1)}, f32[768]{0:T(1024)}, u32[]{:S(2)}) copy-start(f32[768]{0:T(1024)} %param.22) | copy-start | bytes 9220
  167.6 1.6 copy-start.5
  168.4 8.5 copy-start.15
  175.1 5.1 copy-start.19
  175.3 4.9 copy-start.45
  245.4 14.7 %copy-start.26 = (bf16[4,2,320,768]{3,2,1,0:T(8,128)(2,1)}, bf16[4,2,320,768]{3,2,1,0:T(8,128)(2,1)S(1)}, u32[]{:S(2)}) copy-start(bf16[4,2,320,768]{3,2,1,0:T(8,128)(2,1)S(1)} %copy.48) | copy-start | bytes 11796484
  354.9 234.0 %reduce-scatter.16.cloned.1.call-start = ((), (), s32[]{:S(2)}) async-start(), calls=%async_computation.15 | async-start | bytes 2359296
  421.7 30.3 %copy-start.20 = (f32[1024,1,2]{2,1,0:T(1,128)S(1)}, f32[1024,1,2]{2,1,0:T(1,128)}, u32[]{:S(2)}) copy-start(f32[1024,1,2]{2,1,0:T(1,128)} %copy-done.19) | copy-start | bytes 24580
  421.7 30.3 %copy-start.46 = (f32[1024]{0:T(1024)S(1)}, f32[1024]{0:T(1024)}, u32[]{:S(2)}) copy-start(f32[1024]{0:T(1024)} %copy-done.45) | copy-start | bytes 12292
  421.7 30.3 %copy-start.48 = (f32[1024]{0:T(1024)S(1)}, f32[1024]{0:T(1024)}, u32[]{:S(2)}) copy-start(f32[1024]{0:T(1024)} %copy-done.47) | copy-start | bytes 12292
  421.7 31.3 %copy-start.25 = (s32[1024,2]{1,0:T(8,128)S(1)}, s32[1024,2]{1,0:T(8,128)}, u32[]{:S(2)}) copy-start(s32[1024,2]{1,0:T(8,128)} %copy-done.24) | copy-start | bytes 24580
  453.0 6.0 copy-start.50
  453.0 6.0 copy-start.52
  453.1 6.0 copy-start.54
  458.9 5.9 copy-start.34
  458.9 134.0 %reduce-scatter.20.cloned.1.call-start = ((), (), s32[]{:S(2)}) async-start(), calls=%async_computation.17 | async-start | bytes 294912
  459.0 5.7 copy-start.6
  459.0 5.7 copy-start.18
  464.8 2.5 copy-start.33
  465.6 1.6 copy-start.10
  467.2 2.7 copy-start.4
  467.2 2.7 copy-start.8
  467.2 2.7 copy-start.44
  473.9 1.9 copy-start.21
  490.8 5.7 copy-start.1
  490.8 5.7 copy-start.9
  502.4 1.9 copy-start.21
  520.4 5.7 copy-start.1
  520.4 5.7 copy-start.9
  530.1 2.2 copy-start.2
  532.2 2.1 copy-start.40
  532.4 2.9 copy-start.29
  532.4 2.9 copy-start.42
  534.3 2.1 copy-start.31
  541.1 119.0 %reduce-scatter.18.cloned.1.call-start = ((), (), s32[]{:S(2)}) async-start(), calls=%async_computation.16 | async-start | bytes 2359296
  547.5 200.6 %reduce-scatter.14.cloned.1.call-start = ((), (), s32[]{:S(2)}) async-start(), calls=%async_computation.14 | async-start | bytes 10616832 | tf_op jit(solution)/shard_map/reduce_scatter | solution.py:237
  562.9 351.3 %reduce-scatter.12.cloned.1.call-start = ((), (), s32[]{:S(2)}) async-start(), calls=%async_computation.13 | async-start | bytes 10616832 | tf_op jit(solution)/shard_map/reduce_scatter | solution.py:234
  576.6 459.1 %all-reduce.10.cloned.1.call-start = ((), (), s32[]{:S(2)}) async-start(), calls=%async_computation.18 | async-start | bytes 9437184 | tf_op jit(solution)/shard_map/psum | solution.py:221
  576.6 3.5 copy-start.30
  582.5 2.3 copy-start.11
  582.5 2.3 copy-start.23
  588.1 5.8 copy-start.58
  1035.7 2.5 copy-start.38
  1035.7 3.5 copy-start.37
  1035.7 4.5 copy-start.36
  (12 other events, 13.8 us)
Sparse Core Ops, SparseCore 0:
  9.6 29.8 all-gather.2
  41.1 27.2 all-gather.4
  79.4 85.8 all-reduce.5
  355.0 96.6 all-reduce.7
  459.0 26.0 reduce-scatter.15
  541.2 10.9 reduce-scatter.19
  555.1 26.0 reduce-scatter.17
  584.8 163.2 reduce-scatter.13
  751.7 162.5 reduce-scatter.11
  918.7 116.9 all-reduce.9
where the time goes:
time: 1050 us
  waiting for transfers between devices  461 us (44%)
  matrix products  194 us (18%)
  local copies, waits for them, and re-layouts  150 us (14%)
  blocking collectives  128 us (12%)
  other arithmetic  91.3 us (9%)
  between operations  15.2 us (1%)
    reduce_scatter x1, waiting for transfers between devices, local(): lax.psum_scatter(grad_w_in.astype(jnp.bfloat16), 'dp', scatter_dimension=...  163 us
    psum x1, waiting for transfers between devices, local(): lax.psum((grad_w_query, grad_w_key, grad_w_value, grad_w_output, gain_sha...  118 us
    reduce_scatter x1, waiting for transfers between devices, local(): lax.psum_scatter(grad_w_out.astype(jnp.bfloat16), 'dp', scatter_dimension...  83.9 us
    psum x1, blocking collectives, local(): lax.psum((grad_w_query, grad_w_key, grad_w_value, grad_w_output, gain_sha...  66.1 us
    psum x1, waiting for transfers between devices, local(): hidden = residual + lax.psum(attn_part, 'tensor')  63.2 us
    all_gather x1, waiting for transfers between devices, local(): lax.all_gather(tokens, 'tensor', axis=1, tiled=True)  30.8 us
    psum x1, blocking collectives, local(): lax.psum((grad_two_part, gate_grad_part), 'tensor')  28.7 us
    scatter x1, local copies, waits for them, and re-layouts, local(): send = jnp.zeros((experts * capacity, D), bf16).at[place].set(doubled).re...  25 us
  transfers between devices with their start and end apart: 10, of which 5 were waited for; matrix products, arithmetic and copies ran while one was open for 25% of the time, Pallas kernels for 0%

commit v1 on v0

v1 whole, which is shorter than its diff:
```python
import functools
import math

import jax
import jax.numpy as jnp
from jax import lax
from jax.experimental import pallas as pl
from jax.experimental.pallas import tpu as pltpu
from jax.sharding import PartitionSpec as P

D = 768
DH = 64
TOP = 2
epsilon = 1e-06
bf16 = jnp.bfloat16
f32 = jnp.float32
FACTOR = 1.0 / math.sqrt(DH)
QB = 256
CHUNK = 768
ROOT = math.sqrt(2.0 / math.pi)
CUBE = 0.044715


def rms_scale(rows):
    return lax.rsqrt(jnp.mean(rows * rows, axis=-1, keepdims=True) + epsilon)


def dot(a, b, ca=1, cb=0):
    return lax.dot_general(a, b, (((ca,), (cb,)), ((), ())), preferred_element_type=f32)


def causal(rows, cols, start):
    at = start + lax.broadcasted_iota(jnp.int32, (rows, cols), 0)
    return lax.broadcasted_iota(jnp.int32, (rows, cols), 1) <= at


def attend_kernel(q_ref, k_ref, v_ref, o_ref, l_ref):
    seq = q_ref.shape[0]
    for half in range(2):
        cols = slice(half * DH, half * DH + DH)
        for start in range(0, seq, QB):
            end = start + QB
            s = dot(q_ref[start:end, cols], k_ref[:end, cols], 1, 1) * FACTOR
            s = jnp.where(causal(QB, end, start), s, -1e30)
            peak = jnp.max(s, axis=1, keepdims=True)
            expo = jnp.exp(s - peak)
            total = jnp.sum(expo, axis=1, keepdims=True)
            prob = (expo * (1.0 / total)).astype(bf16)
            o_ref[start:end, cols] = dot(prob, v_ref[:end, cols]).astype(bf16)
            l_ref[start:end, cols] = jnp.broadcast_to(peak + jnp.log(total), (QB, DH))


def attend(query, key, value):
    seq, width = query.shape
    spec = pl.BlockSpec((seq, 128), lambda i: (0, i))
    return pl.pallas_call(
        attend_kernel,
        grid=(width // 128,),
        in_specs=[spec] * 3,
        out_specs=[spec] * 2,
        out_shape=[
            jax.ShapeDtypeStruct((seq, width), bf16),
            jax.ShapeDtypeStruct((seq, width), f32),
        ],
        compiler_params=pltpu.CompilerParams(vmem_limit_bytes=48 << 20),
    )(query, key, value)


def back_kernel(q_ref, k_ref, v_ref, o_ref, l_ref, g_ref, dq_ref, dk_ref, dv_ref, ks, vs):
    seq = q_ref.shape[0]
    for half in range(2):
        cols = slice(half * DH, half * DH + DH)
        ks[...] = jnp.zeros_like(ks)
        vs[...] = jnp.zeros_like(vs)
        for start in range(0, seq, QB):
            end = start + QB
            q = q_ref[start:end, cols]
            k = k_ref[:end, cols]
            g = g_ref[start:end, cols]
            s = dot(q, k, 1, 1) * FACTOR
            log_total = l_ref[start:end, half * DH : half * DH + 1]
            prob = jnp.where(causal(QB, end, start), jnp.exp(s - log_total), 0.0)
            gp = dot(g, v_ref[:end, cols], 1, 1)
            inner = jnp.sum(
                g.astype(f32) * o_ref[start:end, cols].astype(f32), axis=1, keepdims=True
            )
            ds = (prob * (gp - inner)).astype(bf16)
            dq_ref[start:end, cols] = (dot(ds, k) * FACTOR).astype(bf16)
            ks[:end] += dot(ds, q, 0, 0)
            vs[:end] += dot(prob.astype(bf16), g, 0, 0)
        dk_ref[:, cols] = (ks[...] * FACTOR).astype(bf16)
        dv_ref[:, cols] = vs[...].astype(bf16)


def attend_back(query, key, value, out, log_total, grad):
    seq, width = query.shape
    spec = pl.BlockSpec((seq, 128), lambda i: (0, i))
    return pl.pallas_call(
        back_kernel,
        grid=(width // 128,),
        in_specs=[spec] * 6,
        out_specs=[spec] * 3,
        out_shape=[jax.ShapeDtypeStruct((seq, width), bf16)] * 3,
        scratch_shapes=[pltpu.VMEM((seq, DH), f32)] * 2,
        compiler_params=pltpu.CompilerParams(vmem_limit_bytes=48 << 20),
    )(query, key, value, out, log_total, grad)


def moe_kernel(
    cap,
    x_ref, dy_ref, pos_ref, gate_ref, wi_ref, wo_ref,
    y_ref, dx_ref, dg_ref, gi_ref, go_ref,
    pick, xin, din, gdin, gcol, eo, dxin,
):
    expert, chunk = pl.program_id(0), pl.program_id(1)
    seq = x_ref.shape[1]

    @pl.when((expert == 0) & (chunk == 0))
    def _():
        y_ref[...] = jnp.zeros_like(y_ref)
        dx_ref[...] = jnp.zeros_like(dx_ref)

    @pl.when(chunk == 0)
    def _():
        dg_ref[...] = jnp.zeros_like(dg_ref)
        eo[...] = jnp.zeros_like(eo)
        dxin[...] = jnp.zeros_like(dxin)
        for s in range(2):
            rows = slice(s * cap, s * cap + cap)
            hit = lax.broadcasted_iota(jnp.int32, (cap, seq), 0) == pos_ref[0, s : s + 1, :]
            gates = jnp.sum(
                jnp.where(hit, gate_ref[0, s : s + 1, :], 0.0), axis=1, keepdims=True
            )
            gcol[rows] = jnp.broadcast_to(gates, (cap, 128))
            mask = jnp.where(hit, 1.0, 0.0).astype(bf16)
            pick[rows] = mask
            xin[rows] = dot(mask, x_ref[s]).astype(bf16)
            moved = dot(mask, dy_ref[s])
            din[rows] = moved.astype(bf16)
            gdin[rows] = (moved * gates).astype(bf16)

    wi = wi_ref[0]
    wo = wo_ref[0]
    for s in range(2):
        rows = slice(s * cap, s * cap + cap)
        gates = gcol[rows, 0:1]
        a = dot(xin[rows], wi)
        u = dot(din[rows], wo, 1, 1)
        t = jnp.tanh(ROOT * (a + CUBE * a * a * a))
        act = 0.5 * a * (1.0 + t)
        slope = 0.5 * (1.0 + t) + 0.5 * a * (1.0 - t * t) * (
            ROOT * (1.0 + 3.0 * CUBE * a * a)
        )
        low_act = act.astype(bf16)
        da = (u * gates * slope).astype(bf16)
        dg = jnp.sum(low_act.astype(f32) * u, axis=1, keepdims=True)
        dg_ref[0, s : s + 1, :] += jnp.sum(
            jnp.where(pick[rows] > 0, dg, 0.0), axis=0, keepdims=True
        )
        eo[rows] += dot(low_act, wo)
        dxin[rows] += dot(da, wi, 1, 1)
        left = dot(xin[rows], da, 0, 0)
        right = dot(gdin[rows], low_act, 0, 0)
        if s == 0:
            gsum_i, gsum_o = left, right
        else:
            gi_ref[0] = (gsum_i + left).astype(bf16)
            go_ref[0] = (gsum_o + right).astype(bf16)

    @pl.when(chunk == pl.num_programs(1) - 1)
    def _():
        for s in range(2):
            rows = slice(s * cap, s * cap + cap)
            mask = pick[rows]
            out = (eo[rows] * gcol[rows, 0:1]).astype(bf16)
            y_ref[s] = (y_ref[s].astype(f32) + dot(mask, out, 0, 0)).astype(bf16)
            back = dxin[rows].astype(bf16)
            dx_ref[s] = (dx_ref[s].astype(f32) + dot(mask, back, 0, 0)).astype(bf16)


def moe(x, dy, pos, gate, w_in, w_out, cap):
    experts, d, hidden = w_in.shape
    seq = x.shape[1]
    whole = pl.BlockSpec((2, seq, d), lambda e, c: (0, 0, 0), pipeline_mode=pl.Buffered(1))
    result = pl.BlockSpec((2, seq, d), lambda e, c: (0, 0, 0))
    small = pl.BlockSpec((1, 2, seq), lambda e, c: (e, 0, 0))
    wide = pl.BlockSpec((1, d, CHUNK), lambda e, c: (e, 0, c))
    tall = pl.BlockSpec((1, CHUNK, d), lambda e, c: (e, c, 0))
    return pl.pallas_call(
        functools.partial(moe_kernel, cap),
        grid=(experts, hidden // CHUNK),
        in_specs=[whole, whole, small, small, wide, tall],
        out_specs=[result, result, small, wide, wide],
        out_shape=[
            jax.ShapeDtypeStruct((2, seq, d), bf16),
            jax.ShapeDtypeStruct((2, seq, d), bf16),
            jax.ShapeDtypeStruct((experts, 2, seq), f32),
            jax.ShapeDtypeStruct((experts, d, hidden), bf16),
            jax.ShapeDtypeStruct((experts, d, hidden), bf16),
        ],
        scratch_shapes=[
            pltpu.VMEM((2 * cap, seq), bf16),
            pltpu.VMEM((2 * cap, d), bf16),
            pltpu.VMEM((2 * cap, d), bf16),
            pltpu.VMEM((2 * cap, d), bf16),
            pltpu.VMEM((2 * cap, 128), f32),
            pltpu.VMEM((2 * cap, d), f32),
            pltpu.VMEM((2 * cap, d), f32),
        ],
        compiler_params=pltpu.CompilerParams(vmem_limit_bytes=60 << 20),
    )(x, dy, pos, gate, w_in, w_out)


def swap(x, axis):
    return lax.ppermute(x, axis, [(0, 1), (1, 0)])


def after(x, *others):
    return lax.optimization_barrier((x, *others))[0]


def joined(mine, theirs, index, axis):
    return jnp.where(
        index == 0,
        jnp.concatenate([mine, theirs], axis),
        jnp.concatenate([theirs, mine], axis),
    )


def split(value):
    high = lax.reduce_precision(value, 8, 7)
    return jnp.concatenate([high.astype(bf16), (value - high).astype(bf16)], 0)


def local(
    n_dp,
    tokens, gain_attn, w_query, w_key, w_value, w_output,
    gain_moe, w_router, w_in, w_out, routes, cotangent,
):
    seq, width = tokens.shape
    tensor = lax.axis_index("tensor")
    core = lax.axis_index("expert")
    dp = lax.axis_index("dp")
    experts = w_router.shape[1]
    mine_experts = w_in.shape[0]
    cap = 5 * TOP * seq // (4 * experts)

    other_tokens = swap(tokens, "tensor")
    other_routes = swap(routes, "expert")
    whole_in = joined(tokens, other_tokens, tensor, 1)
    other_cot = swap(after(cotangent, other_tokens), "tensor")
    other_wo = swap(after(w_output, other_cot), "tensor")

    residual = whole_in.astype(f32)
    scale_one = rms_scale(residual)
    normed_one = residual * scale_one
    low_one = (normed_one * gain_attn).astype(bf16)
    query = dot(low_one, w_query).astype(bf16)
    key = dot(low_one, w_key).astype(bf16)
    value = dot(low_one, w_value).astype(bf16)
    heads_out, log_total = attend(query, key, value)
    other_heads = swap(heads_out, "tensor")

    lanes = jnp.arange(experts, dtype=jnp.int32)[:, None]
    earlier = (
        jnp.arange(seq, dtype=jnp.int32)[:, None] < jnp.arange(seq, dtype=jnp.int32)[None, :]
    ).astype(bf16)

    def places(table):
        named = (table[0:1] == lanes) | (table[1:2] == lanes)
        before = dot(named.astype(bf16), earlier).astype(jnp.int32)
        return jnp.where(named, before, -1)

    table, other_table = routes.T, other_routes.T
    first = core * mine_experts
    pos = jnp.stack(
        [
            lax.dynamic_slice_in_dim(places(table), first, mine_experts, 0),
            lax.dynamic_slice_in_dim(places(other_table), first, mine_experts, 0),
        ],
        1,
    )
    whole_cot = joined(cotangent, other_cot, tensor, 1)
    cots = jnp.stack([whole_cot, swap(whole_cot, "expert")])
    grad_top = whole_cot.astype(f32)
    whole_wo = joined(w_output, other_wo, tensor, 0)

    all_heads = joined(heads_out, other_heads, tensor, 1)
    hidden = residual + dot(all_heads, whole_wo)
    scale_two = rms_scale(hidden)
    normed_two = hidden * scale_two
    low_two = (normed_two * gain_moe).astype(bf16)
    logits = dot(w_router, low_two, 0, 1)
    picks = [(table[j : j + 1] == lanes).astype(f32) for j in range(TOP)]
    chosen = jnp.concatenate([jnp.sum(p * logits, 0, keepdims=True) for p in picks], 0)
    expo = jnp.exp(chosen - jnp.max(chosen, 0, keepdims=True))
    gates = expo / jnp.sum(expo, 0, keepdims=True)
    by_expert = picks[0] * gates[0:1] + picks[1] * gates[1:2]
    other_low = swap(low_two, "expert")
    other_gates = swap(by_expert, "expert")
    gate = jnp.stack(
        [
            lax.dynamic_slice_in_dim(by_expert, first, mine_experts, 0),
            lax.dynamic_slice_in_dim(other_gates, first, mine_experts, 0),
        ],
        1,
    )
    y, dx, dg, grad_w_in, grad_w_out = moe(
        jnp.stack([low_two, other_low]), cots, pos, gate, w_in, w_out, cap
    )

    dx_part = (dx[0].astype(f32) + swap(dx[1], "expert").astype(f32)).astype(bf16)
    dg_part = joined(dg[:, 0], swap(dg[:, 1], "expert"), core, 0)
    dx_other = swap(dx_part, "tensor")
    gate_grad = dg_part + swap(dg_part, "tensor")
    grad_two_sum = dx_part.astype(f32) + dx_other.astype(f32)

    def columns(a, index):
        return lax.dynamic_slice_in_dim(a, index * width, width, 1)

    y_part = (y[0].astype(f32) + swap(after(y[1], dx_part), "expert").astype(f32)).astype(bf16)
    y_other = swap(after(columns(y_part, 1 - tensor), dx_other), "tensor")
    mixed = (
        columns(hidden, tensor) + columns(y_part, tensor).astype(f32) + y_other.astype(f32)
    ).astype(bf16)

    outer = n_dp // 2
    share = D // n_dp
    pairs = [(i, i ^ 1) for i in range(n_dp)]
    groups = [list(range(r, n_dp, 2)) for r in range(2)]
    low_bit = lax.rem(dp, 2)
    ffs = w_in.shape[2]

    def pair_sum(a, axis):
        mine = lax.dynamic_index_in_dim(a, low_bit, axis, keepdims=False)
        send = lax.dynamic_index_in_dim(a, 1 - low_bit, axis, keepdims=False)
        return mine.astype(f32) + lax.ppermute(send, "dp", pairs).astype(f32)

    def line_sum(a):
        return lax.psum_scatter(
            a, "dp", scatter_dimension=1, axis_index_groups=groups, tiled=True
        )

    def shares(a):
        return a.reshape(mine_experts, outer, 2, share, ffs)

    out_half = pair_sum(shares(grad_w_out), 2).astype(bf16)
    in_quarter = line_sum(grad_w_in.reshape(mine_experts, outer, 2 * share, ffs))
    out_share = line_sum(out_half).reshape(mine_experts, share, ffs)
    in_share = pair_sum(in_quarter.reshape(mine_experts, 2, share, ffs), 1)
    grad_in_share = in_share
    grad_out_share = jnp.swapaxes(out_share, 1, 2).astype(f32)

    grads_j = [jnp.sum(p * gate_grad, 0, keepdims=True) for p in picks]
    mean_j = gates[0:1] * grads_j[0] + gates[1:2] * grads_j[1]
    grad_logits = sum(picks[j] * (gates[j : j + 1] * (grads_j[j] - mean_j)) for j in range(TOP))
    parts = split(grad_logits)
    grad_two = grad_two_sum + dot(parts, jnp.concatenate([w_router, w_router], 1), 0, 1)
    router_parts = dot(parts, low_two)
    grad_router = (router_parts[:experts] + router_parts[experts:]).T
    grad_gain_moe = jnp.sum(grad_two * normed_two, axis=0)
    scaled_two = grad_two * gain_moe
    grad_hidden = grad_top + scale_two * (
        scaled_two - normed_two * jnp.mean(normed_two * scaled_two, axis=1, keepdims=True)
    )
    grad_attn = grad_hidden.astype(bf16)
    grad_heads = dot(grad_attn, w_output, 1, 1).astype(bf16)
    grad_w_output = dot(heads_out, grad_attn, 0, 0)
    dq, dk, dv = attend_back(query, key, value, heads_out, log_total, grad_heads)
    grad_qkv = [dot(low_one, g, 0, 0) for g in (dq, dk, dv)]
    grad_one = dot(dq, w_query, 1, 1) + dot(dk, w_key, 1, 1) + dot(dv, w_value, 1, 1)
    gain_part = jnp.sum(grad_one * normed_one, axis=0)
    scaled_one = grad_one * gain_attn
    grad_in_part = scale_one * (
        scaled_one - normed_one * jnp.mean(normed_one * scaled_one, axis=1, keepdims=True)
    )
    theirs = swap(columns(grad_in_part, 1 - tensor).astype(bf16), "tensor")
    grad_tokens = (
        columns(grad_hidden, tensor) + columns(grad_in_part, tensor) + theirs.astype(f32)
    )
    dense = jnp.concatenate([g.astype(bf16) for g in grad_qkv], 1)
    dense = lax.psum(
        jnp.concatenate([dense, grad_w_output.astype(bf16).reshape(D, width)], 1),
        ("dp", "expert"),
    ).astype(f32)
    tiny = lax.psum(
        jnp.concatenate([gain_part, 0.5 * grad_gain_moe, 0.5 * grad_router.reshape(-1)]),
        ("dp", "expert", "tensor"),
    )
    return (
        mixed,
        grad_tokens,
        lax.dynamic_slice_in_dim(tiny[:D], tensor * width, width, 0),
        dense[:, :width],
        dense[:, width : 2 * width],
        dense[:, 2 * width : 3 * width],
        dense[:, 3 * width :].reshape(width, D),
        tiny[D : 2 * D],
        tiny[2 * D :].reshape(D, experts),
        grad_in_share,
        grad_out_share,
    )


def solution(mesh):
    in_specs = (
        P(("dp", "expert"), "tensor"),
        P(),
        P(None, "tensor"),
        P(None, "tensor"),
        P(None, "tensor"),
        P("tensor", None),
        P(),
        P(),
        P("expert", None, "tensor"),
        P("expert", "tensor", None),
        P(("dp", "expert"), None),
        P(("dp", "expert"), "tensor"),
    )
    out_specs = (
        P(("dp", "expert"), "tensor"),
        P(("dp", "expert"), "tensor"),
        P("tensor"),
        P(None, "tensor"),
        P(None, "tensor"),
        P(None, "tensor"),
        P("tensor", None),
        P(),
        P(),
        P("expert", "dp", "tensor"),
        P("expert", "tensor", "dp"),
    )
    return jax.shard_map(
        functools.partial(local, mesh.shape["dp"]),
        mesh=mesh,
        in_specs=in_specs,
        out_specs=out_specs,
        check_vma=False,
    )
```

time: 1050 us -> 532 us (0.51)
  waiting for transfers between devices: 461 us -> 194 us
  matrix products: 194 us -> 27.4 us
  Pallas kernels: 0 us -> 118 us
  local copies, waits for them, and re-layouts: 150 us -> 46.9 us
  blocking collectives: 128 us -> 72.4 us
  other arithmetic: 91.3 us -> 36.4 us
  starting transfers between devices: 0.41 us -> 16.2 us
    reduce_scatter x2, waiting for transfers between devices: 247 us -> 0.01 us  [line_sum(): lax.psum_scatter(a, 'dp', scatter_dimension=1, axis_index_groups=groups,...]
    dot_general x37 -> x17, matrix products: 194 us -> 27.4 us  [dot(): lax.dot_general(a, b, (((ca,), (cb,)), ((), ())), preferred_element_type=...]
    pallas_call x0 -> x3, Pallas kernels: none -> 118 us  [the longest x1 84.2 us: moe(): pl.pallas_call(functools.partial(moe_kernel, cap), grid=(experts, hidden...]
    ppermute x0 -> x17, waiting for transfers between devices: none -> 115 us  [the longest x15 73 us: swap(): return lax.ppermute(x, axis, [(0, 1), (1, 0)])]
    psum x3 -> x1, waiting for transfers between devices: 182 us -> 79.2 us  [local(): lax.psum(jnp.concatenate([dense, grad_w_output.astype(bf16).reshape(D, wi...]
    reduce_sum x7 -> x2, other arithmetic: 36.7 us -> 0.06 us  [the longest x1 0.03 us: local(): gates = expo / jnp.sum(expo, 0, keepdims=True)]
    all_to_all x4 -> x0, blocking collectives: 33.6 us -> none  [the longest x1 10.1 us: local(): lax.all_to_all(grad_arrived_part, 'expert', split_axis=1, concat_axis=0,...]
    all_gather x2 -> x0, waiting for transfers between devices: 30.8 us -> none  [the longest x1 30.8 us: local(): lax.all_gather(tokens, 'tensor', axis=1, tiled=True)]
  transfers between devices with their start and end apart: 10 -> 20, of which waited for: 5 -> 10; matrix products, arithmetic and copies ran while one was open for 25% -> 18% of each run, Pallas kernels for 0% -> 6%
where the time goes in v1:
time: 532 us; the launch traced here: 528 us
  waiting for transfers between devices  194 us (36%)
  Pallas kernels  118 us (22%)
  blocking collectives  72.4 us (14%)
  local copies, waits for them, and re-layouts  46.9 us (9%)
  other arithmetic  36.4 us (7%)
  matrix products  27.4 us (5%)
  between operations  16.6 us (3%)
  starting transfers between devices  16.2 us (3%)
    pallas_call x1, Pallas kernels, moe(): pl.pallas_call(functools.partial(moe_kernel, cap), grid=(experts, hidden...  84.2 us
    psum x1, waiting for transfers between devices, local(): lax.psum(jnp.concatenate([dense, grad_w_output.astype(bf16).reshape(D, wi...  79.2 us
    ppermute x15, waiting for transfers between devices, swap(): return lax.ppermute(x, axis, [(0, 1), (1, 0)])  73 us
    psum x1, blocking collectives, local(): lax.psum(jnp.concatenate([gain_part, 0.5 * grad_gain_moe, 0.5 * grad_rout...  72.4 us
    ppermute x2, waiting for transfers between devices, pair_sum(): return mine.astype(f32) + lax.ppermute(send, 'dp', pairs).astype(f32)  41.9 us
    dot_general x17, matrix products, dot(): lax.dot_general(a, b, (((ca,), (cb,)), ((), ())), preferred_element_type=...  27.4 us
    pallas_call x1, Pallas kernels, attend_back(): pl.pallas_call(back_kernel, grid=(width // 128,), in_specs=[spec] * 6, ou...  19.3 us
    pallas_call x1, Pallas kernels, attend(): pl.pallas_call(attend_kernel, grid=(width // 128,), in_specs=[spec] * 3,...  14.2 us
  transfers between devices with their start and end apart: 20, of which 10 were waited for; matrix products, arithmetic and copies ran while one was open for 18% of the time, Pallas kernels for 6%

profile of v1, /device:TPU:0, one launch (start us, length us, event | category | flops | bytes accessed | tf_op | source)
XLA Modules:
  0.0 527.9 jit_solution(8173856464649940213)
XLA Ops:
  8.1 3.0 collective-permute-start
  11.1 0.8 fusion.59
  12.5 16.4 %collective-permute-done = bf16[1024,384]{1,0:T(8,128)(2,1)S(1)} collective-permute-done((bf16[1024,384]{1,0:T(8,128)(2,1)}, bf16[1024,384]{1,0:T(8,128)(2,1)S(1)}, u32[]{:S(2)}, u32[]{:S(2)}) %collective-permute-start) | collective-permute-done | bytes 786464 | tf_op jit(solution)/shard_map/ppermute | solution.py:215
  28.8 1.7 collective-permute-start.2
  30.6 2.0 fusion.12
  32.6 2.7 convolution_convert_fusion.3.q_ref
  35.4 1.1 convolution_convert_fusion.2.k_ref
  36.5 2.5 convolution_convert_fusion.1.v_ref
  39.1 14.2 %shard_map.203 = (bf16[1024,384]{1,0:T(8,128)(2,1)S(1)}, f32[1024,384]{1,0:T(8,128)S(1)}) custom-call(bf16[1024,384]{1,0:T(8,128)(2,1)S(1)} %convolution_convert_fusion.3.q_ref, bf16[1024,384]{1,0:T(8,128)(2,1)S(1)} %convolution_convert_fusion.2.k_ref, bf16[1024,384]{1,0:T(8,128)(2,1)S(1)} %convolution_convert_fusion.1.v_ref), custom_call_target="tpu_custom_call" | custom-call | tf_op jit(solution)/shard_map/pallas_call | solution.py:56
  53.9 1.8 collective-permute-start.3
  57.3 16.5 %collective-permute-done.1 = bf16[1024,384]{1,0:T(8,128)(2,1)S(1)} collective-permute-done((bf16[1024,384]{1,0:T(8,128)(2,1)S(1)}, bf16[1024,384]{1,0:T(8,128)(2,1)S(1)}, u32[]{:S(2)}, u32[]{:S(2)}) %collective-permute-start.1) | collective-permute-done | bytes 786464 | tf_op jit(solution)/shard_map/ppermute | solution.py:215
  73.8 10.3 %collective-permute-done.3 = bf16[384,768]{1,0:T(8,128)(2,1)S(1)} collective-permute-done((bf16[384,768]{1,0:T(8,128)(2,1)S(1)}, bf16[384,768]{1,0:T(8,128)(2,1)S(1)}, u32[]{:S(2)}, u32[]{:S(2)}) %collective-permute-start.3) | collective-permute-done | bytes 589856 | tf_op jit(solution)/shard_map/ppermute | solution.py:215
  84.1 1.7 multiply_reduce_fusion.2
  88.0 1.7 collective-permute-done.7
  90.4 2.0 pad_maximum_fusion.1.dy_ref
  92.4 1.9 pad_maximum_fusion.x_ref
  94.3 84.2 %shard_map.204 = (bf16[2,1024,768]{2,1,0:T(8,128)(2,1)}, bf16[2,1024,768]{2,1,0:T(8,128)(2,1)}, f32[4,2,1024]{2,1,0:T(2,128)}, bf16[4,768,1536]{2,1,0:T(8,128)(2,1)}, bf16[4,768,1536]{2,1,0:T(8,128)(2,1)}) custom-call(bf16[2,1024,768]{2,1,0:T(8,128)(2,1)} %pad_maximum_fusion.x_ref, bf16[2,1024,768]{2,1,0:T(8,128)(2,1)} %pad_maximum_fusion.1.dy_ref, ...), custom_call_target="tpu_custom_call" | custom-call | tf_op jit(solution)/shard_map/pallas_call | solution.py:189
  178.5 8.2 %copy.47 = bf16[4,4,192,1536]{3,2,0,1:T(8,128)(2,1)} copy(bf16[4,4,192,1536]{3,2,1,0:T(8,128)(2,1)} %bitcast.78) | data formatting | bytes 18874368 | tf_op jit(solution)/shard_map/reshape | solution.py:348
  186.9 2.7 slice_bitcast_fusion
  189.7 3.6 collective-permute-done.8
  193.3 3.7 fusion.13
  197.0 1.2 collective-permute-start.10
  198.2 6.7 %constant_dynamic-slice_fusion = (bf16[4,4,1,96,1536]{4,3,2,1,0:T(8,128)(2,1)}, bf16[4,4,1,96,1536]{4,3,2,1,0:T(8,128)(2,1)S(1)}) fusion(bf16[4,4,2,96,1536]{4,3,2,1,0:T(8,128)(2,1)} %bitcast.77, s32[]{:T(128)S(6)} %select_n.92, s32[]{:T(128)S(6)} %select_n.93), kind=kLoop, calls=%fused_computation.112 | loop fusion | bytes 18874376 | tf_op jit(solution)/shard_map/jit(dynamic_index_in_dim)/dynamic_slice | solution.py:335
  204.8 2.5 copy.62
  207.4 1.4 collective-permute-start.16
  208.9 1.2 collective-permute-done.12
  210.1 1.2 collective-permute-start.13
  211.3 23.1 %collective-permute-done.13 = f32[8,1024]{1,0:T(8,128)S(1)} collective-permute-done((f32[8,1024]{1,0:T(8,128)S(1)}, f32[8,1024]{1,0:T(8,128)S(1)}, u32[]{:S(2)}, u32[]{:S(2)}) %collective-permute-start.13) | collective-permute-done | bytes 32800 | tf_op jit(solution)/shard_map/ppermute | solution.py:215
  234.6 4.9 multiply_reduce_fusion
  239.5 0.8 multiply_add_fusion
  240.3 1.7 copy-done.13
  242.0 0.8 convolution_convert_fusion.4
  242.9 1.0 reshape.153
  243.9 1.3 copy.45
  245.2 4.0 convolution_convert_fusion.g_ref
  249.2 19.3 %shard_map.205 = (bf16[1024,384]{1,0:T(8,128)(2,1)S(1)}, bf16[1024,384]{1,0:T(8,128)(2,1)S(1)}, bf16[1024,384]{1,0:T(8,128)(2,1)S(1)}) custom-call(bf16[1024,384]{1,0:T(8,128)(2,1)S(1)} %convolution_convert_fusion.3.q_ref, bf16[1024,384]{1,0:T(8,128)(2,1)S(1)} %convolution_convert_fusion.2.k_ref, bf16[1024,384]{1,0:T(8,128)(2,1)S(1)} %convolution_convert_fusion.1.v_ref, ...), custom_call_target="tpu_custom_call" | custom-call | tf_op jit(solution)/shard_map/pallas_call | solution.py:98
  268.6 1.0 convolution_convert_fusion.5
  269.7 1.0 convolution_convert_fusion.6
  270.7 1.0 convolution_convert_fusion.7
  271.7 1.6 pad_maximum_fusion.2
  273.6 41.9 %collective-permute-done.16 = bf16[4,4,96,1536]{3,2,0,1:T(8,128)(2,1)} collective-permute-done((bf16[4,4,96,1536]{3,2,0,1:T(8,128)(2,1)}, bf16[4,4,96,1536]{3,2,0,1:T(8,128)(2,1)}, u32[]{:S(2)}, u32[]{:S(2)}) %collective-permute-start.16) | collective-permute-done | bytes 4718624 | tf_op jit(solution)/shard_map/ppermute | solution.py:337
  315.5 7.6 %fusion = bf16[4,4,96,1536]{3,2,0,1:T(8,128)(2,1)} fusion(bf16[4,4,96,1536]{3,2,0,1:T(8,128)(2,1)} %collective-permute-done.16, bf16[4,4,1,96,1536]{4,3,2,1,0:T(8,128)(2,1)} %get-tuple-element.80), kind=kLoop, calls=%fused_computation.1 | loop fusion | flops 9437184 | bytes 14155776 | tf_op jit(solution)/shard_map/convert_element_type | solution.py:347
  323.1 2.8 slice_bitcast_fusion.1
  325.9 1.8 fusion.40
  328.2 1.0 fusion.61
  329.3 1.0 fusion.62
  330.9 1.7 fusion.11
  332.5 1.2 fusion.10
  333.8 1.1 dynamic-slice_convert_fusion
  334.9 1.0 collective-permute-start.14
  336.5 1.1 collective-permute-start.11
  337.6 72.4 %psum.14 = f32[7680]{0:T(1024)S(1)} all-reduce(f32[7680]{0:T(1024)S(1)} %pad_maximum_fusion.5), channel_id=1, replica_groups=mesh['dp'=8,'expert'=2,'tensor'=2] {'dp','expert','tensor'}, use_global_device_ids=true, to_apply=%region_11.12 | all-reduce | flops 7680 | bytes 61440 | tf_op jit(solution)/shard_map/psum | solution.py:386
  412.2 3.5 convert_add_fusion.5
  415.7 2.4 dynamic-slice_bitcast_fusion
  418.1 2.3 collective-permute-start.15
  420.3 2.8 add_convert_fusion
  423.1 79.2 %all-reduce.2.cloned.1.call-done = bf16[768,1536]{0,1:T(8,128)(2,1)} async-done(((bf16[768,1536]{0,1:T(8,128)(2,1)}), bf16[768,1536]{0,1:T(8,128)(2,1)}) %all-reduce.2.cloned.1.call-update) | async-done | bytes 2359312 | tf_op jit(solution)/shard_map/psum | solution.py:382
  502.3 3.4 fusion.56
  505.7 2.7 copy.50
  508.3 2.7 copy.51
  511.0 1.4 copy.52
  512.7 1.3 reshape.154
  514.1 3.1 convert_bitcast_fusion
  517.2 3.0 convert_add_fusion.4
  (162 shorter events, 10.8 us)
Async XLA Ops:
  8.0 28.5 %copy-start = (bf16[768,384]{1,0:T(8,128)(2,1)S(1)}, bf16[768,384]{1,0:T(8,128)(2,1)}, u32[]{:S(2)}) copy-start(bf16[768,384]{1,0:T(8,128)(2,1)} %param.16) | copy-start | bytes 1769476
  8.0 407.7 %reduce-scatter.3.cloned.1.call-start = ((), (), s32[]{:S(2)}) async-start(), calls=%async_computation.3 | async-start | bytes 11796480 | tf_op jit(solution)/shard_map/reduce_scatter | solution.py:340
  8.1 20.8 %collective-permute-start = (bf16[1024,384]{1,0:T(8,128)(2,1)}, bf16[1024,384]{1,0:T(8,128)(2,1)S(1)}, u32[]{:S(2)}, u32[]{:S(2)}) collective-permute-start(bf16[1024,384]{1,0:T(8,128)(2,1)} %param.12), channel_id=1, source_target_pairs={{0,1},{1,0},{2,3},{3,2},{4,5},{5,4},{6,7},{7,6},{8,9},{9,8},{10,11... | collective-permute-start | bytes 2359304 | tf_op jit(solution)/shard_map/ppermute | solution.py:215
  11.1 1.4 collective-permute-start.6
  28.8 6.6 %copy-start.21 = (bf16[1024,384]{1,0:T(8,128)(2,1)}, bf16[1024,384]{1,0:T(8,128)(2,1)S(1)}, u32[]{:S(2)}) copy-start(bf16[1024,384]{1,0:T(8,128)(2,1)S(1)} %collective-permute-done) | copy-start | bytes 2359300
  28.8 25.1 %collective-permute-start.2 = (bf16[1024,384]{1,0:T(8,128)(2,1)}, bf16[1024,384]{1,0:T(8,128)(2,1)S(1)}, u32[]{:S(2)}, u32[]{:S(2)}) collective-permute-start(bf16[1024,384]{1,0:T(8,128)(2,1)} %param.23), channel_id=1, source_target_pairs={{0,1},{1,0},{2,3},{3,2},{4,5},{5,4},{6,7},{7,6},{8,9},{9,8},{10,11... | collective-permute-start | bytes 2359304 | tf_op jit(solution)/shard_map/ppermute | solution.py:215
  32.6 3.9 copy-start.38
  32.6 2.8 copy-start.18
  32.6 2.8 copy-start.30
  32.6 2.8 copy-start.41
  39.1 14.9 %copy-start.28 = (bf16[384,768]{1,0:T(8,128)(2,1)S(1)}, bf16[384,768]{1,0:T(8,128)(2,1)}, u32[]{:S(2)}) copy-start(bf16[384,768]{1,0:T(8,128)(2,1)} %param.17) | copy-start | bytes 1769476
  39.1 17.4 %copy-start.26 = (bf16[1024,384]{1,0:T(8,128)(2,1)S(1)}, bf16[1024,384]{1,0:T(8,128)(2,1)}, u32[]{:S(2)}) copy-start(bf16[1024,384]{1,0:T(8,128)(2,1)} %param.23) | copy-start | bytes 2359300
  53.2 4.0 copy-start.4
  53.3 30.8 %copy-start.1 = (bf16[1024,384]{1,0:T(8,128)(2,1)}, bf16[1024,384]{1,0:T(8,128)(2,1)S(1)}, u32[]{:S(2)}) copy-start(bf16[1024,384]{1,0:T(8,128)(2,1)S(1)} %get-tuple-element.25.o_ref) | copy-start | bytes 2359300
  53.3 20.5 %collective-permute-start.1 = (bf16[1024,384]{1,0:T(8,128)(2,1)S(1)}, bf16[1024,384]{1,0:T(8,128)(2,1)S(1)}, u32[]{:S(2)}, u32[]{:S(2)}) collective-permute-start(bf16[1024,384]{1,0:T(8,128)(2,1)S(1)} %get-tuple-element.25.o_ref), channel_id=1, source_target_pairs={{0,1},{1,0},{2,3},{3,2},{4,5},{5,4},{6,7},{7,6},{8,9},{9,8},{10,11... | collective-permute-start | bytes 2359304 | tf_op jit(solution)/shard_map/ppermute | solution.py:215
  53.9 30.2 %collective-permute-start.3 = (bf16[384,768]{1,0:T(8,128)(2,1)S(1)}, bf16[384,768]{1,0:T(8,128)(2,1)S(1)}, u32[]{:S(2)}, u32[]{:S(2)}) collective-permute-start(bf16[384,768]{1,0:T(8,128)(2,1)S(1)} %copy-done.28), channel_id=1, source_target_pairs={{0,1},{1,0},{2,3},{3,2},{4,5},{5,4},{6,7},{7,6},{8,9},{9,8},{10,11... | collective-permute-start | bytes 1769480 | tf_op jit(solution)/shard_map/ppermute | solution.py:215
  56.4 27.7 %copy-start.22 = (bf16[1024,384]{1,0:T(8,128)(2,1)S(1)}, bf16[1024,384]{1,0:T(8,128)(2,1)}, u32[]{:S(2)}) copy-start(bf16[1024,384]{1,0:T(8,128)(2,1)} %copy-done.21) | copy-start | bytes 2359300
  56.8 29.0 %copy-start.16 = (bf16[1024,768]{1,0:T(8,128)(2,1)}, bf16[1024,768]{1,0:T(8,128)(2,1)S(1)}, u32[]{:S(2)}) copy-start(bf16[1024,768]{1,0:T(8,128)(2,1)S(1)} %maximum_select_fusion.4) | copy-start | bytes 4718596
  56.8 33.6 %collective-permute-start.5 = (bf16[1024,768]{1,0:T(8,128)(2,1)S(1)}, bf16[1024,768]{1,0:T(8,128)(2,1)S(1)}, u32[]{:S(2)}, u32[]{:S(2)}) collective-permute-start(bf16[1024,768]{1,0:T(8,128)(2,1)S(1)} %maximum_select_fusion.4), channel_id=1, source_target_pairs={{0,2},{2,0},{1,3},{3,1},{4,6},{6,4},{5,7},{7,5},{8,10},{10,8},{9,1... | collective-permute-start | bytes 4718600 | tf_op jit(solution)/shard_map/ppermute | solution.py:215
  57.3 28.6 %copy-start.35 = (f32[768]{0:T(1024)S(1)}, f32[768]{0:T(1024)}, u32[]{:S(2)}) copy-start(f32[768]{0:T(1024)} %param.18) | copy-start | bytes 9220
  85.8 1.7 copy-start.11
  85.8 0.7 copy-start.36
  86.2 1.8 copy-start.14
  86.2 6.2 %collective-permute-start.4 = (bf16[1024,768]{1,0:T(8,128)(2,1)S(1)}, bf16[1024,768]{1,0:T(8,128)(2,1)S(1)}, u32[]{:S(2)}, u32[]{:S(2)}) collective-permute-start(bf16[1024,768]{1,0:T(8,128)(2,1)S(1)} %multiply_convert_fusion), channel_id=1, source_target_pairs={{0,2},{2,0},{1,3},{3,1},{4,6},{6,4},{5,7},{7,5},{8,10},{10,8},{9,1... | collective-permute-start | bytes 4718600 | tf_op jit(solution)/shard_map/ppermute | solution.py:215
  87.2 2.5 collective-permute-start.7
  186.7 315.6 %all-reduce.2.cloned.1.call-start = ((), (), s32[]{:S(2)}) async-start(), calls=%async_computation.2 | async-start | bytes 4718592 | tf_op jit(solution)/shard_map/psum | solution.py:382
  189.6 3.8 collective-permute-start.8
  197.0 37.5 %collective-permute-start.10 = (bf16[1024,768]{1,0:T(8,128)(2,1)}, bf16[1024,768]{1,0:T(8,128)(2,1)}, u32[]{:S(2)}, u32[]{:S(2)}) collective-permute-start(bf16[1024,768]{1,0:T(8,128)(2,1)} %fusion.13), channel_id=1, source_target_pairs={{0,1},{1,0},{2,3},{3,2},{4,5},{5,4},{6,7},{7,6},{8,9},{9,8},{10,11... | collective-permute-start | bytes 4718600 | tf_op jit(solution)/shard_map/ppermute | solution.py:215
  204.8 4.0 copy-start.34
  207.4 108.1 %collective-permute-start.16 = (bf16[4,4,96,1536]{3,2,0,1:T(8,128)(2,1)}, bf16[4,4,96,1536]{3,2,0,1:T(8,128)(2,1)}, u32[]{:S(2)}, u32[]{:S(2)}) collective-permute-start(bf16[4,4,96,1536]{3,2,0,1:T(8,128)(2,1)} %bitcast.75), channel_id=1, source_target_pairs={{0,4},{4,0},{8,12},{12,8},{16,20},{20,16},{24,28},{28,24},{1,5},{5... | collective-permute-start | bytes 14155784 | tf_op jit(solution)/shard_map/ppermute | solution.py:337
  208.8 1.2 collective-permute-start.12
  210.1 24.3 %collective-permute-start.13 = (f32[8,1024]{1,0:T(8,128)S(1)}, f32[8,1024]{1,0:T(8,128)S(1)}, u32[]{:S(2)}, u32[]{:S(2)}) collective-permute-start(f32[8,1024]{1,0:T(8,128)S(1)} %maximum_select_fusion.7), channel_id=1, source_target_pairs={{0,1},{1,0},{2,3},{3,2},{4,5},{5,4},{6,7},{7,6},{8,9},{9,8},{10,11... | collective-permute-start | bytes 98312 | tf_op jit(solution)/shard_map/ppermute | solution.py:215
  234.5 5.0 copy-start.32
  234.5 4.9 copy-start.12
  234.6 4.9 copy-start.17
  239.5 2.5 copy-start.2
  240.3 1.7 copy-start.13
  245.2 4.0 copy-start.3
  249.2 19.4 %copy-start.19 = (bf16[1024,384]{1,0:T(8,128)(2,1)S(1)}, bf16[1024,384]{1,0:T(8,128)(2,1)}, u32[]{:S(2)}) copy-start(bf16[1024,384]{1,0:T(8,128)(2,1)} %param.12) | copy-start | bytes 2359300
  249.2 19.4 %copy-start.23 = (bf16[1024,384]{1,0:T(8,128)(2,1)S(1)}, bf16[1024,384]{1,0:T(8,128)(2,1)}, u32[]{:S(2)}) copy-start(bf16[1024,384]{1,0:T(8,128)(2,1)} %copy-done.21) | copy-start | bytes 2359300
  249.2 19.4 %copy-start.39 = (f32[1024]{0:T(1024)S(1)}, f32[1024]{0:T(1024)}, u32[]{:S(2)}) copy-start(f32[1024]{0:T(1024)} %copy-done.38) | copy-start | bytes 12292
  249.2 19.4 %copy-start.42 = (f32[768]{0:T(1024)S(1)}, f32[768]{0:T(1024)}, u32[]{:S(2)}) copy-start(f32[768]{0:T(1024)} %param.13) | copy-start | bytes 9220
  268.5 1.1 copy-start.9
  268.5 1.1 copy-start.5
  268.6 2.1 copy-start.7
  273.3 240.8 %reduce-scatter.5.cloned.1.call-start = ((), (), s32[]{:S(2)}) async-start(), calls=%async_computation.4 | async-start | bytes 5898240 | tf_op jit(solution)/shard_map/reduce_scatter | solution.py:340
  323.1 2.8 copy-start.33
  323.1 5.1 copy-start.8
  323.1 5.1 copy-start.29
  325.9 3.3 copy-start.6
  328.1 1.1 copy-start.31
  328.1 7.8 %collective-permute-start.9 = (bf16[1024,768]{1,0:T(8,128)(2,1)}, bf16[1024,768]{1,0:T(8,128)(2,1)S(1)}, u32[]{:S(2)}, u32[]{:S(2)}) collective-permute-start(bf16[1024,768]{1,0:T(8,128)(2,1)} %slice_bitcast_fusion.1), channel_id=1, source_target_pairs={{0,2},{2,0},{1,3},{3,1},{4,6},{6,4},{5,7},{7,5},{8,10},{10,8},{9,1... | collective-permute-start | bytes 4718600 | tf_op jit(solution)/shard_map/ppermute | solution.py:215
  329.2 1.1 copy-start.10
  329.2 1.4 copy-start.20
  329.2 1.6 copy-start.24
  329.3 1.6 copy-start.40
  329.3 1.6 copy-start.43
  332.5 3.3 copy-start.25
  333.7 2.6 copy-start.15
  334.9 2.7 copy-start.37
  334.9 77.4 %collective-permute-start.14 = (bf16[1024,384]{1,0:T(8,128)(2,1)}, bf16[1024,384]{1,0:T(8,128)(2,1)}, u32[]{:S(2)}, u32[]{:S(2)}) collective-permute-start(bf16[1024,384]{1,0:T(8,128)(2,1)} %dynamic-slice_convert_fusion), channel_id=1, source_target_pairs={{0,1},{1,0},{2,3},{3,2},{4,5},{5,4},{6,7},{7,6},{8,9},{9,8},{10,11... | collective-permute-start | bytes 2359304 | tf_op jit(solution)/shard_map/ppermute | solution.py:215
  336.5 83.9 %collective-permute-start.11 = (bf16[1024,384]{1,0:T(8,128)(2,1)S(1)}, bf16[1024,384]{1,0:T(8,128)(2,1)}, u32[]{:S(2)}, u32[]{:S(2)}) collective-permute-start(bf16[1024,384]{1,0:T(8,128)(2,1)S(1)} %constant_dynamic-slice_fusion.1), channel_id=1, source_target_pairs={{0,1},{1,0},{2,3},{3,2},{4,5},{5,4},{6,7},{7,6},{8,9},{9,8},{10,11... | collective-permute-start | bytes 2359304 | tf_op jit(solution)/shard_map/ppermute | solution.py:215
  418.1 99.1 %collective-permute-start.15 = (bf16[4,96,1536]{2,1,0:T(8,128)(2,1)}, bf16[4,96,1536]{2,1,0:T(8,128)(2,1)}, u32[]{:S(2)}, u32[]{:S(2)}) collective-permute-start(bf16[4,96,1536]{2,1,0:T(8,128)(2,1)} %dynamic-slice_bitcast_fusion), channel_id=1, source_target_pairs={{0,4},{4,0},{8,12},{12,8},{16,20},{20,16},{24,28},{28,24},{1,5},{5... | collective-permute-start | bytes 3538952 | tf_op jit(solution)/shard_map/ppermute | solution.py:337
  514.1 3.1 copy-start.27
Sparse Core Ops, SparseCore 0:
  186.8 165.8 reduce-scatter.2
  355.0 90.0 reduce-scatter.4
Sparse Core Ops, SparseCore 1:
  273.4 228.8 all-reduce.1

commit v2 on v1

--- a/solution.py
+++ b/solution.py
@@ -164,8 +164,9 @@
         if s == 0:
             gsum_i, gsum_o = left, right
         else:
-            gi_ref[0] = (gsum_i + left).astype(bf16)
-            go_ref[0] = (gsum_o + right).astype(bf16)
+            tile = (gi_ref.shape[0],) + gi_ref.shape[2:]
+            gi_ref[:, 0] = (gsum_i + left).astype(bf16).reshape(tile)
+            go_ref[:, 0] = (gsum_o + right).astype(bf16).reshape(tile)
 
     @pl.when(chunk == pl.num_programs(1) - 1)
     def _():
@@ -178,25 +179,28 @@
             dx_ref[s] = (dx_ref[s].astype(f32) + dot(mask, back, 0, 0)).astype(bf16)
 
 
-def moe(x, dy, pos, gate, w_in, w_out, cap):
-    experts, d, hidden = w_in.shape
+def moe(x, dy, pos, gate, w_in, w_out, cap, begin, experts, outer):
+    _, d, hidden = w_in.shape
+    split_rows = d // outer
     seq = x.shape[1]
     whole = pl.BlockSpec((2, seq, d), lambda e, c: (0, 0, 0), pipeline_mode=pl.Buffered(1))
     result = pl.BlockSpec((2, seq, d), lambda e, c: (0, 0, 0))
-    small = pl.BlockSpec((1, 2, seq), lambda e, c: (e, 0, 0))
-    wide = pl.BlockSpec((1, d, CHUNK), lambda e, c: (e, 0, c))
-    tall = pl.BlockSpec((1, CHUNK, d), lambda e, c: (e, c, 0))
+    small = pl.BlockSpec((1, 2, seq), lambda e, c: (begin + e, 0, 0))
+    wide = pl.BlockSpec((1, d, CHUNK), lambda e, c: (begin + e, 0, c))
+    tall = pl.BlockSpec((1, CHUNK, d), lambda e, c: (begin + e, c, 0))
+    small_out = pl.BlockSpec((1, 2, seq), lambda e, c: (e, 0, 0))
+    graded = pl.BlockSpec((outer, 1, split_rows, CHUNK), lambda e, c: (0, e, 0, c))
     return pl.pallas_call(
         functools.partial(moe_kernel, cap),
         grid=(experts, hidden // CHUNK),
         in_specs=[whole, whole, small, small, wide, tall],
-        out_specs=[result, result, small, wide, wide],
+        out_specs=[result, result, small_out, graded, graded],
         out_shape=[
             jax.ShapeDtypeStruct((2, seq, d), bf16),
             jax.ShapeDtypeStruct((2, seq, d), bf16),
             jax.ShapeDtypeStruct((experts, 2, seq), f32),
-            jax.ShapeDtypeStruct((experts, d, hidden), bf16),
-            jax.ShapeDtypeStruct((experts, d, hidden), bf16),
+            jax.ShapeDtypeStruct((outer, experts, split_rows, hidden), bf16),
+            jax.ShapeDtypeStruct((outer, experts, split_rows, hidden), bf16),
         ],
         scratch_shapes=[
             pltpu.VMEM((2 * cap, seq), bf16),
@@ -305,51 +309,74 @@
         ],
         1,
     )
-    y, dx, dg, grad_w_in, grad_w_out = moe(
-        jnp.stack([low_two, other_low]), cots, pos, gate, w_in, w_out, cap
-    )
-
-    dx_part = (dx[0].astype(f32) + swap(dx[1], "expert").astype(f32)).astype(bf16)
-    dg_part = joined(dg[:, 0], swap(dg[:, 1], "expert"), core, 0)
-    dx_other = swap(dx_part, "tensor")
-    gate_grad = dg_part + swap(dg_part, "tensor")
-    grad_two_sum = dx_part.astype(f32) + dx_other.astype(f32)
-
-    def columns(a, index):
-        return lax.dynamic_slice_in_dim(a, index * width, width, 1)
-
-    y_part = (y[0].astype(f32) + swap(after(y[1], dx_part), "expert").astype(f32)).astype(bf16)
-    y_other = swap(after(columns(y_part, 1 - tensor), dx_other), "tensor")
-    mixed = (
-        columns(hidden, tensor) + columns(y_part, tensor).astype(f32) + y_other.astype(f32)
-    ).astype(bf16)
-
     outer = n_dp // 2
     share = D // n_dp
     pairs = [(i, i ^ 1) for i in range(n_dp)]
     groups = [list(range(r, n_dp, 2)) for r in range(2)]
     low_bit = lax.rem(dp, 2)
     ffs = w_in.shape[2]
-
-    def pair_sum(a, axis):
-        mine = lax.dynamic_index_in_dim(a, low_bit, axis, keepdims=False)
-        send = lax.dynamic_index_in_dim(a, 1 - low_bit, axis, keepdims=False)
-        return mine.astype(f32) + lax.ppermute(send, "dp", pairs).astype(f32)
+    some = mine_experts // 2
+
+    def halves(a):
+        a = a.reshape(a.shape[0], some, 2, share, ffs)
+        mine = lax.dynamic_index_in_dim(a, low_bit, 2, keepdims=False)
+        return mine, lax.dynamic_index_in_dim(a, 1 - low_bit, 2, keepdims=False)
+
+    def pair(send):
+        return lax.ppermute(send, "dp", pairs).astype(f32)
 
     def line_sum(a):
         return lax.psum_scatter(
-            a, "dp", scatter_dimension=1, axis_index_groups=groups, tiled=True
+            a, "dp", scatter_dimension=0, axis_index_groups=groups, tiled=True
         )
 
-    def shares(a):
-        return a.reshape(mine_experts, outer, 2, share, ffs)
-
-    out_half = pair_sum(shares(grad_w_out), 2).astype(bf16)
-    in_quarter = line_sum(grad_w_in.reshape(mine_experts, outer, 2 * share, ffs))
-    out_share = line_sum(out_half).reshape(mine_experts, share, ffs)
-    in_share = pair_sum(in_quarter.reshape(mine_experts, 2, share, ffs), 1)
-    grad_in_share = in_share
-    grad_out_share = jnp.swapaxes(out_share, 1, 2).astype(f32)
+    both = jnp.stack([low_two, other_low])
+    y_a, dx_a, dg_a, gi_a, go_a = moe(
+        both, cots, pos, gate, w_in, w_out, cap, 0, some, outer
+    )
+    go_a_mine, go_a_send = halves(go_a)
+    gi_a_line = line_sum(gi_a)
+    y_b, dx_b, dg_b, gi_b, go_b = moe(
+        after(both, go_a_send), cots, pos, gate, w_in, w_out, cap, some, some, outer
+    )
+    go_a_pair = pair(go_a_send)
+
+    dx_part = (
+        dx_a[0].astype(f32)
+        + dx_b[0].astype(f32)
+        + swap(dx_a[1], "expert").astype(f32)
+        + swap(dx_b[1], "expert").astype(f32)
+    ).astype(bf16)
+    dg = jnp.concatenate([dg_a, dg_b], 0)
+    dg_part = joined(dg[:, 0], swap(dg[:, 1], "expert"), core, 0)
+    dx_other = swap(dx_part, "tensor")
+    gate_grad = dg_part + swap(dg_part, "tensor")
+    grad_two_sum = dx_part.astype(f32) + dx_other.astype(f32)
+
+    gi_b, go_b = lax.optimization_barrier((gi_b, go_b, dx_part))[:2]
+    gi_b_mine, gi_b_send = halves(gi_b)
+    go_b_mine, go_b_send = halves(go_b)
+    gi_b_pair = pair(after(gi_b_send, go_a_pair))
+    go_a_half = (go_a_mine.astype(f32) + go_a_pair).astype(bf16)
+    go_a_line = line_sum(go_a_half)
+    go_b_pair = pair(after(go_b_send, gi_b_pair))
+    gi_b_line = line_sum((gi_b_mine.astype(f32) + gi_b_pair).astype(bf16))
+    go_b_half = (go_b_mine.astype(f32) + go_b_pair).astype(bf16)
+    go_b_line = line_sum(go_b_half)
+
+    def columns(a, index):
+        return lax.dynamic_slice_in_dim(a, index * width, width, 1)
+
+    y_part = (
+        y_a[0].astype(f32)
+        + y_b[0].astype(f32)
+        + swap(y_a[1], "expert").astype(f32)
+        + swap(after(y_b[1], dx_part), "expert").astype(f32)
+    ).astype(bf16)
+    y_other = swap(after(columns(y_part, 1 - tensor), dx_other), "tensor")
+    mixed = (
+        columns(hidden, tensor) + columns(y_part, tensor).astype(f32) + y_other.astype(f32)
+    ).astype(bf16)
 
     grads_j = [jnp.sum(p * gate_grad, 0, keepdims=True) for p in picks]
     mean_j = gates[0:1] * grads_j[0] + gates[1:2] * grads_j[1]
@@ -378,25 +405,30 @@
     grad_tokens = (
         columns(grad_hidden, tensor) + columns(grad_in_part, tensor) + theirs.astype(f32)
     )
-    dense = jnp.concatenate([g.astype(bf16) for g in grad_qkv], 1)
-    dense = lax.psum(
-        jnp.concatenate([dense, grad_w_output.astype(bf16).reshape(D, width)], 1),
-        ("dp", "expert"),
-    ).astype(f32)
-    tiny = lax.psum(
-        jnp.concatenate([gain_part, 0.5 * grad_gain_moe, 0.5 * grad_router.reshape(-1)]),
-        ("dp", "expert", "tensor"),
-    )
+    gain_row = gain_part[None]
+    gain_share = columns(gain_row, tensor) + swap(columns(gain_row, 1 - tensor), "tensor")
+    tiny = jnp.concatenate([gain_share[0], grad_gain_moe, grad_router.reshape(-1)])
+    grad_qkv[2] = jnp.concatenate([grad_qkv[2], tiny.reshape(-1, width)], 0)
+    dense = [g.astype(bf16) for g in grad_qkv + [grad_w_output]]
+    dense = lax.optimization_barrier((*dense, go_b_half))[:-1]
+    dense = [g.astype(f32) for g in lax.psum(dense, ("dp", "expert"))]
+    tiny = dense[2][D:].reshape(-1)
+
+    gi_a_mine, gi_a_send = halves(gi_a_line)
+    gi_a_share = (gi_a_mine.astype(f32) + pair(gi_a_send))[0]
+    grad_in_share = jnp.concatenate([gi_a_share, gi_b_line[0].astype(f32)], 0)
+    grad_out_share = jnp.concatenate([go_a_line[0], go_b_line[0]], 0)
+    grad_out_share = jnp.swapaxes(grad_out_share, 1, 2).astype(f32)
     return (
         mixed,
         grad_tokens,
-        lax.dynamic_slice_in_dim(tiny[:D], tensor * width, width, 0),
-        dense[:, :width],
-        dense[:, width : 2 * width],
-        dense[:, 2 * width : 3 * width],
-        dense[:, 3 * width :].reshape(width, D),
-        tiny[D : 2 * D],
-        tiny[2 * D :].reshape(D, experts),
+        tiny[:width],
+        dense[0],
+        dense[1],
+        dense[2][:D],
+        dense[3],
+        tiny[width : width + D],
+        tiny[width + D :].reshape(D, experts),
         grad_in_share,
         grad_out_share,
     )

time: 532 us -> 615 us (1.16)
  waiting for transfers between devices: 194 us -> 350 us
  blocking collectives: 72.4 us -> 0 us
  local copies, waits for them, and re-layouts: 46.9 us -> 26.6 us
  other arithmetic: 36.4 us -> 45.5 us
  Pallas kernels: 118 us -> 125 us
    ppermute x2 -> x4, waiting for transfers between devices: 41.9 us -> 128 us  [pair(): return lax.ppermute(send, 'dp', pairs).astype(f32)]
    psum x1 -> x0, blocking collectives: 72.4 us -> none  [local(): lax.psum(jnp.concatenate([gain_part, 0.5 * grad_gain_moe, 0.5 * grad_rout...]
    ppermute x15 -> x18, waiting for transfers between devices: 73 us -> 120 us  [swap(): return lax.ppermute(x, axis, [(0, 1), (1, 0)])]
    psum x1, waiting for transfers between devices: 79.2 us -> 101 us  [local(): dense = [g.astype(f32) for g in lax.psum(dense, ('dp', 'expert'))]]
    convert_element_type x4 -> x11, other arithmetic: 14.9 us -> 28 us  [the longest x1 4.74 us: local(): dx_part = (dx_a[0].astype(f32) + dx_b[0].astype(f32) + swap(dx_a[1], 'exp...]
    reshape x5 -> x3, local copies, waits for them, and re-layouts: 12 us -> 0.45 us  [the longest x1 0.22 us: local(): tiny[width + D:].reshape(D, experts)]
    squeeze x4 -> x7, local copies, waits for them, and re-layouts: 7.78 us -> 18 us  [the longest x3 9.47 us: halves(): return (mine, lax.dynamic_index_in_dim(a, 1 - low_bit, 2, keepdims=False))]
    dynamic_slice x3 -> x0, local copies, waits for them, and re-layouts: 9.85 us -> none  [the longest x1 6.67 us: pair_sum(): mine = lax.dynamic_index_in_dim(a, low_bit, axis, keepdims=False)]
  transfers between devices with their start and end apart: 20 -> 27, of which waited for: 10 -> 14; matrix products, arithmetic and copies ran while one was open for 18% -> 14% of each run, Pallas kernels for 6% -> 13%
where the time goes in v2:
time: 615 us; the launch traced here: 611 us
  waiting for transfers between devices  350 us (57%)
  Pallas kernels  125 us (20%)
  other arithmetic  45.5 us (7%)
  matrix products  27.3 us (4%)
  local copies, waits for them, and re-layouts  26.6 us (4%)
  starting transfers between devices  19.2 us (3%)
  between operations  16.7 us (3%)
    ppermute x4, waiting for transfers between devices, pair(): return lax.ppermute(send, 'dp', pairs).astype(f32)  128 us
    ppermute x18, waiting for transfers between devices, swap(): return lax.ppermute(x, axis, [(0, 1), (1, 0)])  120 us
    psum x1, waiting for transfers between devices, local(): dense = [g.astype(f32) for g in lax.psum(dense, ('dp', 'expert'))]  101 us
    pallas_call x2, Pallas kernels, moe(): pl.pallas_call(functools.partial(moe_kernel, cap), grid=(experts, hidden...  92 us
    dot_general x17, matrix products, dot(): lax.dot_general(a, b, (((ca,), (cb,)), ((), ())), preferred_element_type=...  27.3 us
    pallas_call x1, Pallas kernels, attend_back(): pl.pallas_call(back_kernel, grid=(width // 128,), in_specs=[spec] * 6, ou...  19.4 us
    pallas_call x1, Pallas kernels, attend(): pl.pallas_call(attend_kernel, grid=(width // 128,), in_specs=[spec] * 3,...  14 us
    ppermute x18, starting transfers between devices, swap(): return lax.ppermute(x, axis, [(0, 1), (1, 0)])  13.2 us
  transfers between devices with their start and end apart: 27, of which 14 were waited for; matrix products, arithmetic and copies ran while one was open for 14% of the time, Pallas kernels for 13%

profile of v2, /device:TPU:0, one launch (start us, length us, event | category | flops | bytes accessed | tf_op | source)
XLA Modules:
  0.0 610.6 jit_solution(16424528773526231113)
XLA Ops:
  8.6 2.6 collective-permute-start
  12.4 17.1 %collective-permute-done = bf16[1024,384]{1,0:T(8,128)(2,1)S(1)} collective-permute-done((bf16[1024,384]{1,0:T(8,128)(2,1)}, bf16[1024,384]{1,0:T(8,128)(2,1)S(1)}, u32[]{:S(2)}, u32[]{:S(2)}) %collective-permute-start) | collective-permute-done | bytes 786464 | tf_op jit(solution)/shard_map/ppermute | solution.py:219
  29.5 2.2 fusion.14
  31.7 1.8 collective-permute-start.2
  33.6 2.4 convolution_convert_fusion.1.v_ref
  37.1 2.4 convolution_convert_fusion.3.q_ref
  39.6 14.0 %shard_map.203 = (bf16[1024,384]{1,0:T(8,128)(2,1)S(1)}, f32[1024,384]{1,0:T(8,128)S(1)}) custom-call(bf16[1024,384]{1,0:T(8,128)(2,1)S(1)} %convolution_convert_fusion.3.q_ref, bf16[1024,384]{1,0:T(8,128)(2,1)S(1)} %convolution_convert_fusion.2.k_ref, bf16[1024,384]{1,0:T(8,128)(2,1)S(1)} %convolution_convert_fusion.1.v_ref), custom_call_target="tpu_custom_call" | custom-call | tf_op jit(solution)/shard_map/pallas_call | solution.py:56
  54.3 1.8 collective-permute-start.3
  57.6 16.5 %collective-permute-done.1 = bf16[1024,384]{1,0:T(8,128)(2,1)S(1)} collective-permute-done((bf16[1024,384]{1,0:T(8,128)(2,1)S(1)}, bf16[1024,384]{1,0:T(8,128)(2,1)S(1)}, u32[]{:S(2)}, u32[]{:S(2)}) %collective-permute-start.1) | collective-permute-done | bytes 786464 | tf_op jit(solution)/shard_map/ppermute | solution.py:219
  74.2 11.0 %collective-permute-done.3 = bf16[384,768]{1,0:T(8,128)(2,1)S(1)} collective-permute-done((bf16[384,768]{1,0:T(8,128)(2,1)S(1)}, bf16[384,768]{1,0:T(8,128)(2,1)S(1)}, u32[]{:S(2)}, u32[]{:S(2)}) %collective-permute-start.3) | collective-permute-done | bytes 589856 | tf_op jit(solution)/shard_map/ppermute | solution.py:219
  85.2 1.7 multiply_reduce_fusion.2
  89.1 1.7 collective-permute-done.7
  91.5 2.0 pad_maximum_fusion.1.dy_ref
  93.5 1.9 pad_maximum_fusion.x_ref
  95.4 45.8 %shard_map.204 = (bf16[2,1024,768]{2,1,0:T(8,128)(2,1)}, bf16[2,1024,768]{2,1,0:T(8,128)(2,1)}, f32[2,2,1024]{2,1,0:T(2,128)}, bf16[4,2,192,1536]{3,2,1,0:T(8,128)(2,1)}, bf16[4,2,192,1536]{3,2,1,0:T(8,128)(2,1)}) custom-call(bf16[2,1024,768]{2,1,0:T(8,128)(2,1)} %pad_maximum_fusion.x_ref, bf16[2,1024,768]{2,1,0:T(8,128)(2,1)} %pad_maximum_fusion.1.dy_ref, ...), custom_call_target="tpu_custom_call" | custom-call | tf_op jit(solution)/shard_map/pallas_call | solution.py:193
  141.2 2.7 slice_bitcast_fusion.1
  144.0 3.2 dynamic-slice_bitcast_fusion.2
  147.2 46.2 %shard_map.205 = (bf16[2,1024,768]{2,1,0:T(8,128)(2,1)}, bf16[2,1024,768]{2,1,0:T(8,128)(2,1)}, f32[2,2,1024]{2,1,0:T(2,128)}, bf16[4,2,192,1536]{3,2,1,0:T(8,128)(2,1)}, bf16[4,2,192,1536]{3,2,1,0:T(8,128)(2,1)}) custom-call(bf16[2,1024,768]{2,1,0:T(8,128)(2,1)} %pad_maximum_fusion.x_ref, bf16[2,1024,768]{2,1,0:T(8,128)(2,1)} %pad_maximum_fusion.1.dy_ref, ...), custom_call_target="tpu_custom_call" | custom-call | tf_op jit(solution)/shard_map/pallas_call | solution.py:193
  193.5 2.7 slice_bitcast_fusion
  196.8 3.1 collective-permute-done.10
  199.9 4.7 fusion.16
  205.3 1.5 collective-permute-start.15
  206.8 35.5 %collective-permute-done.15 = f32[8,1024]{1,0:T(8,128)S(1)} collective-permute-done((f32[8,1024]{1,0:T(8,128)S(1)}, f32[8,1024]{1,0:T(8,128)S(1)}, u32[]{:S(2)}, u32[]{:S(2)}) %collective-permute-start.15) | collective-permute-done | bytes 32800 | tf_op jit(solution)/shard_map/ppermute | solution.py:219
  242.3 1.7 fusion.44
  244.4 5.1 dynamic-slice_bitcast_fusion
  249.6 1.5 collective-permute-start.20
  251.1 3.3 multiply_reduce_fusion
  255.5 1.9 convolution_convert_fusion.g_ref
  257.4 19.4 %shard_map.206 = (bf16[1024,384]{1,0:T(8,128)(2,1)S(1)}, bf16[1024,384]{1,0:T(8,128)(2,1)S(1)}, bf16[1024,384]{1,0:T(8,128)(2,1)S(1)}) custom-call(bf16[1024,384]{1,0:T(8,128)(2,1)S(1)} %convolution_convert_fusion.3.q_ref, bf16[1024,384]{1,0:T(8,128)(2,1)S(1)} %convolution_convert_fusion.2.k_ref, bf16[1024,384]{1,0:T(8,128)(2,1)S(1)} %convolution_convert_fusion.1.v_ref, ...), custom_call_target="tpu_custom_call" | custom-call | tf_op jit(solution)/shard_map/pallas_call | solution.py:98
  279.2 3.0 fusion.13
  282.9 1.9 convolution_convert_fusion.7
  284.8 1.9 convolution_convert_fusion.6
  286.8 1.1 convolution_convert_fusion.5
  287.9 1.6 convolution_convert_fusion.4
  290.5 12.2 %collective-permute-done.20 = bf16[4,2,96,1536]{3,2,1,0:T(8,128)(2,1)} collective-permute-done((bf16[4,2,96,1536]{3,2,1,0:T(8,128)(2,1)}, bf16[4,2,96,1536]{3,2,1,0:T(8,128)(2,1)}, u32[]{:S(2)}, u32[]{:S(2)}) %collective-permute-start.20) | collective-permute-done | bytes 2359328 | tf_op jit(solution)/shard_map/ppermute | solution.py:326
  302.7 4.5 fusion.6
  307.8 1.6 collective-permute-start.18
  309.4 55.4 %collective-permute-done.18 = bf16[4,2,96,1536]{3,2,1,0:T(8,128)(2,1)S(1)} collective-permute-done((bf16[4,2,96,1536]{3,2,1,0:T(8,128)(2,1)}, bf16[4,2,96,1536]{3,2,1,0:T(8,128)(2,1)S(1)}, u32[]{:S(2)}, u32[]{:S(2)}) %collective-permute-start.18) | collective-permute-done | bytes 2359328 | tf_op jit(solution)/shard_map/ppermute | solution.py:326
  364.8 3.7 fusion.4
  369.2 1.2 collective-permute-start.19
  370.4 1.5 slice_bitcast_fusion.3
  372.0 50.6 %collective-permute-done.19 = bf16[4,2,96,1536]{3,2,1,0:T(8,128)(2,1)S(1)} collective-permute-done((bf16[4,2,96,1536]{3,2,1,0:T(8,128)(2,1)}, bf16[4,2,96,1536]{3,2,1,0:T(8,128)(2,1)S(1)}, u32[]{:S(2)}, u32[]{:S(2)}) %collective-permute-start.19) | collective-permute-done | bytes 2359328 | tf_op jit(solution)/shard_map/ppermute | solution.py:326
  422.5 3.8 fusion.5
  426.4 1.7 slice_bitcast_fusion.2
  428.1 3.4 collective-permute-done.11
  431.5 2.8 fusion.18
  435.0 1.4 fusion.12
  436.6 1.5 collective-permute-start.16
  438.1 16.7 %collective-permute-done.13 = bf16[1024,384]{1,0:T(8,128)(2,1)S(1)} collective-permute-done((bf16[1024,384]{1,0:T(8,128)(2,1)S(1)}, bf16[1024,384]{1,0:T(8,128)(2,1)S(1)}, u32[]{:S(2)}, u32[]{:S(2)}) %collective-permute-start.13) | collective-permute-done | bytes 786464 | tf_op jit(solution)/shard_map/ppermute | solution.py:219
  454.8 1.2 add_convert_fusion
  456.0 14.9 %collective-permute-done.16 = bf16[1024,384]{1,0:T(8,128)(2,1)S(1)} collective-permute-done((bf16[1024,384]{1,0:T(8,128)(2,1)S(1)}, bf16[1024,384]{1,0:T(8,128)(2,1)S(1)}, u32[]{:S(2)}, u32[]{:S(2)}) %collective-permute-start.16) | collective-permute-done | bytes 786464 | tf_op jit(solution)/shard_map/ppermute | solution.py:219
  470.9 1.4 convert_add_fusion.4
  472.3 100.9 %all-reduce.3.cloned.1.call-done = (bf16[787,384]{1,0:T(8,128)(2,1)}, bf16[768,384]{1,0:T(8,128)(2,1)}, bf16[768,384]{1,0:T(8,128)(2,1)}, bf16[384,768]{1,0:T(8,128)(2,1)}) async-done(((bf16[787,384]{1,0:T(8,128)(2,1)}, bf16[768,384]{1,0:T(8,128)(2,1)}, bf16[768,384]{1,0:T(8,128)(2,1)}, bf16[384,768]{1,0:T(8,128)(2,1)}), (bf16[787,384]{1,0:T(8,128)(2,1)}, bf16[768,384]{1,0:T(8,128)(2,1)}, ...) | async-done | bytes 2373904 | tf_op jit(solution)/shard_map/psum | solution.py:414
  574.7 2.2 slice.118
  576.9 1.2 convert_element_type.225
  579.7 1.1 convert_element_type.226
  580.8 1.1 convert_element_type.227
  583.6 1.1 dynamic-slice_bitcast_fusion.3
  584.7 1.5 collective-permute-start.21
  586.2 2.8 convert_bitcast_fusion
  589.0 1.2 bitcast_convert_fusion
  590.3 9.7 %collective-permute-done.21 = bf16[1,2,96,1536]{3,2,1,0:T(8,128)(2,1)S(1)} collective-permute-done((bf16[1,2,96,1536]{3,2,1,0:T(8,128)(2,1)S(1)}, bf16[1,2,96,1536]{3,2,1,0:T(8,128)(2,1)S(1)}, u32[]{:S(2)}, u32[]{:S(2)}) %collective-permute-start.21) | collective-permute-done | bytes 589856 | tf_op jit(solution)/shard_map/ppermute | solution.py:326
  600.0 1.2 fusion.30
  601.2 1.6 pad_maximum_fusion.2
  (169 shorter events, 21.6 us)
Async XLA Ops:
  8.0 25.6 %copy-start = (bf16[768,384]{1,0:T(8,128)(2,1)S(1)}, bf16[768,384]{1,0:T(8,128)(2,1)}, u32[]{:S(2)}) copy-start(bf16[768,384]{1,0:T(8,128)(2,1)} %param.16) | copy-start | bytes 1769476
  8.0 565.2 %all-reduce.3.cloned.1.call-start = ((), (), s32[]{:S(2)}) async-start(), calls=%async_computation.8 | async-start | bytes 4755456 | tf_op jit(solution)/shard_map/psum | solution.py:414
  8.1 4.3 collective-permute-start.6
  8.6 20.9 %collective-permute-start = (bf16[1024,384]{1,0:T(8,128)(2,1)}, bf16[1024,384]{1,0:T(8,128)(2,1)S(1)}, u32[]{:S(2)}, u32[]{:S(2)}) collective-permute-start(bf16[1024,384]{1,0:T(8,128)(2,1)} %param.12), channel_id=1, source_target_pairs={{0,1},{1,0},{2,3},{3,2},{4,5},{5,4},{6,7},{7,6},{8,9},{9,8},{10,11... | collective-permute-start | bytes 2359304 | tf_op jit(solution)/shard_map/ppermute | solution.py:219
  29.5 6.5 %copy-start.15 = (bf16[1024,384]{1,0:T(8,128)(2,1)}, bf16[1024,384]{1,0:T(8,128)(2,1)S(1)}, u32[]{:S(2)}) copy-start(bf16[1024,384]{1,0:T(8,128)(2,1)S(1)} %collective-permute-done) | copy-start | bytes 2359300
  31.7 4.3 copy-start.13
  31.7 4.3 copy-start.24
  31.7 4.3 copy-start.35
  31.7 22.6 %collective-permute-start.2 = (bf16[1024,384]{1,0:T(8,128)(2,1)}, bf16[1024,384]{1,0:T(8,128)(2,1)S(1)}, u32[]{:S(2)}, u32[]{:S(2)}) collective-permute-start(bf16[1024,384]{1,0:T(8,128)(2,1)} %param.23), channel_id=1, source_target_pairs={{0,1},{1,0},{2,3},{3,2},{4,5},{5,4},{6,7},{7,6},{8,9},{9,8},{10,11... | collective-permute-start | bytes 2359304 | tf_op jit(solution)/shard_map/ppermute | solution.py:219
  36.0 1.1 copy-start.26
  39.5 14.8 %copy-start.22 = (bf16[384,768]{1,0:T(8,128)(2,1)S(1)}, bf16[384,768]{1,0:T(8,128)(2,1)}, u32[]{:S(2)}) copy-start(bf16[384,768]{1,0:T(8,128)(2,1)} %param.17) | copy-start | bytes 1769476
  39.5 17.3 %copy-start.21 = (bf16[1024,384]{1,0:T(8,128)(2,1)S(1)}, bf16[1024,384]{1,0:T(8,128)(2,1)}, u32[]{:S(2)}) copy-start(bf16[1024,384]{1,0:T(8,128)(2,1)} %param.23) | copy-start | bytes 2359300
  53.6 4.0 copy-start.4
  53.6 31.6 %copy-start.2 = (bf16[1024,384]{1,0:T(8,128)(2,1)}, bf16[1024,384]{1,0:T(8,128)(2,1)S(1)}, u32[]{:S(2)}) copy-start(bf16[1024,384]{1,0:T(8,128)(2,1)S(1)} %get-tuple-element.39.o_ref) | copy-start | bytes 2359300
  53.6 20.5 %collective-permute-start.1 = (bf16[1024,384]{1,0:T(8,128)(2,1)S(1)}, bf16[1024,384]{1,0:T(8,128)(2,1)S(1)}, u32[]{:S(2)}, u32[]{:S(2)}) collective-permute-start(bf16[1024,384]{1,0:T(8,128)(2,1)S(1)} %get-tuple-element.39.o_ref), channel_id=1, source_target_pairs={{0,1},{1,0},{2,3},{3,2},{4,5},{5,4},{6,7},{7,6},{8,9},{9,8},{10,11... | collective-permute-start | bytes 2359304 | tf_op jit(solution)/shard_map/ppermute | solution.py:219
  54.3 30.8 %collective-permute-start.3 = (bf16[384,768]{1,0:T(8,128)(2,1)S(1)}, bf16[384,768]{1,0:T(8,128)(2,1)S(1)}, u32[]{:S(2)}, u32[]{:S(2)}) collective-permute-start(bf16[384,768]{1,0:T(8,128)(2,1)S(1)} %copy-done.22), channel_id=1, source_target_pairs={{0,1},{1,0},{2,3},{3,2},{4,5},{5,4},{6,7},{7,6},{8,9},{9,8},{10,11... | collective-permute-start | bytes 1769480 | tf_op jit(solution)/shard_map/ppermute | solution.py:219
  56.8 28.4 %copy-start.16 = (bf16[1024,384]{1,0:T(8,128)(2,1)S(1)}, bf16[1024,384]{1,0:T(8,128)(2,1)}, u32[]{:S(2)}) copy-start(bf16[1024,384]{1,0:T(8,128)(2,1)} %copy-done.15) | copy-start | bytes 2359300
  57.2 29.7 %copy-start.11 = (bf16[1024,768]{1,0:T(8,128)(2,1)}, bf16[1024,768]{1,0:T(8,128)(2,1)S(1)}, u32[]{:S(2)}) copy-start(bf16[1024,768]{1,0:T(8,128)(2,1)S(1)} %maximum_select_fusion.4) | copy-start | bytes 4718596
  57.2 34.3 %collective-permute-start.5 = (bf16[1024,768]{1,0:T(8,128)(2,1)S(1)}, bf16[1024,768]{1,0:T(8,128)(2,1)S(1)}, u32[]{:S(2)}, u32[]{:S(2)}) collective-permute-start(bf16[1024,768]{1,0:T(8,128)(2,1)S(1)} %maximum_select_fusion.4), channel_id=1, source_target_pairs={{0,2},{2,0},{1,3},{3,1},{4,6},{6,4},{5,7},{7,5},{8,10},{10,8},{9,1... | collective-permute-start | bytes 4718600 | tf_op jit(solution)/shard_map/ppermute | solution.py:219
  57.6 29.3 %copy-start.31 = (f32[768]{0:T(1024)S(1)}, f32[768]{0:T(1024)}, u32[]{:S(2)}) copy-start(f32[768]{0:T(1024)} %param.18) | copy-start | bytes 9220
  86.9 1.7 copy-start.5
  86.9 0.7 copy-start.32
  87.3 1.8 copy-start.10
  87.3 6.2 %collective-permute-start.4 = (bf16[1024,768]{1,0:T(8,128)(2,1)S(1)}, bf16[1024,768]{1,0:T(8,128)(2,1)S(1)}, u32[]{:S(2)}, u32[]{:S(2)}) collective-permute-start(bf16[1024,768]{1,0:T(8,128)(2,1)S(1)} %multiply_convert_fusion), channel_id=1, source_target_pairs={{0,2},{2,0},{1,3},{3,1},{4,6},{6,4},{5,7},{7,5},{8,10},{10,8},{9,1... | collective-permute-start | bytes 4718600 | tf_op jit(solution)/shard_map/ppermute | solution.py:219
  88.3 2.5 collective-permute-start.7
  143.9 52.9 %collective-permute-start.9 = (bf16[1024,768]{1,0:T(8,128)(2,1)}, bf16[1024,768]{1,0:T(8,128)(2,1)}, u32[]{:S(2)}, u32[]{:S(2)}) collective-permute-start(bf16[1024,768]{1,0:T(8,128)(2,1)} %slice_bitcast_fusion.1), channel_id=1, source_target_pairs={{0,2},{2,0},{1,3},{3,1},{4,6},{6,4},{5,7},{7,5},{8,10},{10,8},{9,1... | collective-permute-start | bytes 4718600 | tf_op jit(solution)/shard_map/ppermute | solution.py:219
  193.4 3.1 copy-start.33
  193.5 3.1 copy-start.34
  196.1 3.8 collective-permute-start.10
  196.6 8.7 %collective-permute-start.14 = (f32[4,1024]{1,0:T(4,128)S(1)}, f32[4,1024]{1,0:T(4,128)S(1)}, u32[]{:S(2)}, u32[]{:S(2)}) collective-permute-start(f32[4,1024]{1,0:T(4,128)S(1)} %bitcast.139), channel_id=1, source_target_pairs={{0,2},{2,0},{1,3},{3,1},{4,6},{6,4},{5,7},{7,5},{8,10},{10,8},{9,1... | collective-permute-start | bytes 49160 | tf_op jit(solution)/shard_map/ppermute | solution.py:219
  204.6 46.4 %collective-permute-start.12 = (bf16[1024,768]{1,0:T(8,128)(2,1)}, bf16[1024,768]{1,0:T(8,128)(2,1)}, u32[]{:S(2)}, u32[]{:S(2)}) collective-permute-start(bf16[1024,768]{1,0:T(8,128)(2,1)} %fusion.16), channel_id=1, source_target_pairs={{0,1},{1,0},{2,3},{3,2},{4,5},{5,4},{6,7},{7,6},{8,9},{9,8},{10,11... | collective-permute-start | bytes 4718600 | tf_op jit(solution)/shard_map/ppermute | solution.py:219
  205.3 37.0 %collective-permute-start.15 = (f32[8,1024]{1,0:T(8,128)S(1)}, f32[8,1024]{1,0:T(8,128)S(1)}, u32[]{:S(2)}, u32[]{:S(2)}) collective-permute-start(f32[8,1024]{1,0:T(8,128)S(1)} %maximum_select_fusion.7), channel_id=1, source_target_pairs={{0,1},{1,0},{2,3},{3,2},{4,5},{5,4},{6,7},{7,6},{8,9},{9,8},{10,11... | collective-permute-start | bytes 98312 | tf_op jit(solution)/shard_map/ppermute | solution.py:219
  244.4 6.7 %copy-start.6 = (f32[1024,768]{1,0:T(8,128)S(1)}, f32[1024,768]{1,0:T(8,128)}, u32[]{:S(2)}) copy-start(f32[1024,768]{1,0:T(8,128)} %copy-done.5) | copy-start | bytes 9437188
  249.6 4.8 copy-start.12
  249.6 53.1 %collective-permute-start.20 = (bf16[4,2,96,1536]{3,2,1,0:T(8,128)(2,1)}, bf16[4,2,96,1536]{3,2,1,0:T(8,128)(2,1)}, u32[]{:S(2)}, u32[]{:S(2)}) collective-permute-start(bf16[4,2,96,1536]{3,2,1,0:T(8,128)(2,1)} %get-tuple-element.61), channel_id=1, source_target_pairs={{0,4},{4,0},{8,12},{12,8},{16,20},{20,16},{24,28},{28,24},{1,5},{5... | collective-permute-start | bytes 7077896 | tf_op jit(solution)/shard_map/ppermute | solution.py:326
  254.4 1.1 copy-start.23
  255.5 32.4 %copy-start.8 = (f32[1024,768]{1,0:T(8,128)}, f32[1024,768]{1,0:T(8,128)S(1)}, u32[]{:S(2)}) copy-start(f32[1024,768]{1,0:T(8,128)S(1)} %multiply_add_fusion) | copy-start | bytes 9437188
  255.5 1.9 copy-start.3
  257.4 19.4 %copy-start.25 = (bf16[768,384]{1,0:T(8,128)(2,1)S(1)}, bf16[768,384]{1,0:T(8,128)(2,1)}, u32[]{:S(2)}) copy-start(bf16[768,384]{1,0:T(8,128)(2,1)} %param.15) | copy-start | bytes 1769476
  276.8 1.1 copy-start.27
  277.8 1.1 copy-start.14
  277.9 1.4 copy-start.17
  282.3 7.2 %collective-permute-start.17 = (f32[1,384]{1,0:T(1,128)S(1)}, f32[1,384]{1,0:T(1,128)S(1)}, u32[]{:S(2)}, u32[]{:S(2)}) collective-permute-start(f32[1,384]{1,0:T(1,128)S(1)} %dynamic_slice.74), channel_id=1, source_target_pairs={{0,1},{1,0},{2,3},{3,2},{4,5},{5,4},{6,7},{7,6},{8,9},{9,8},{10,11... | collective-permute-start | bytes 4616 | tf_op jit(solution)/shard_map/ppermute | solution.py:219
  307.2 276.4 %reduce-scatter.5.cloned.1.call-start = ((), (), s32[]{:S(2)}) async-start(), calls=%async_computation.4 | async-start | bytes 5898240 | tf_op jit(solution)/shard_map/reduce_scatter | solution.py:329
  307.8 278.5 %reduce-scatter.9.cloned.1.call-start = ((), (), s32[]{:S(2)}) async-start(), calls=%async_computation.6 | async-start | bytes 2949120 | tf_op jit(solution)/shard_map/reduce_scatter | solution.py:329
  307.8 57.0 %collective-permute-start.18 = (bf16[4,2,96,1536]{3,2,1,0:T(8,128)(2,1)}, bf16[4,2,96,1536]{3,2,1,0:T(8,128)(2,1)S(1)}, u32[]{:S(2)}, u32[]{:S(2)}) collective-permute-start(bf16[4,2,96,1536]{3,2,1,0:T(8,128)(2,1)} %dynamic-slice_bitcast_fusion.2), channel_id=1, source_target_pairs={{0,4},{4,0},{8,12},{12,8},{16,20},{20,16},{24,28},{28,24},{1,5},{5... | collective-permute-start | bytes 7077896 | tf_op jit(solution)/shard_map/ppermute | solution.py:326
  368.6 217.7 %reduce-scatter.11.cloned.1.call-start = ((), (), s32[]{:S(2)}) async-start(), calls=%async_computation.7 | async-start | bytes 2949120 | tf_op jit(solution)/shard_map/reduce_scatter | solution.py:329
  369.1 219.9 %reduce-scatter.7.cloned.1.call-start = ((), (), s32[]{:S(2)}) async-start(), calls=%async_computation.5 | async-start | bytes 2949120 | tf_op jit(solution)/shard_map/reduce_scatter | solution.py:329
  369.2 53.4 %collective-permute-start.19 = (bf16[4,2,96,1536]{3,2,1,0:T(8,128)(2,1)}, bf16[4,2,96,1536]{3,2,1,0:T(8,128)(2,1)S(1)}, u32[]{:S(2)}, u32[]{:S(2)}) collective-permute-start(bf16[4,2,96,1536]{3,2,1,0:T(8,128)(2,1)} %get-tuple-element.60), channel_id=1, source_target_pairs={{0,4},{4,0},{8,12},{12,8},{16,20},{20,16},{24,28},{28,24},{1,5},{5... | collective-permute-start | bytes 7077896 | tf_op jit(solution)/shard_map/ppermute | solution.py:326
  371.9 56.2 %collective-permute-start.8 = (bf16[1024,768]{1,0:T(8,128)(2,1)S(1)}, bf16[1024,768]{1,0:T(8,128)(2,1)}, u32[]{:S(2)}, u32[]{:S(2)}) collective-permute-start(bf16[1024,768]{1,0:T(8,128)(2,1)S(1)} %slice_bitcast_fusion.3), channel_id=1, source_target_pairs={{0,2},{2,0},{1,3},{3,1},{4,6},{6,4},{5,7},{7,5},{8,10},{10,8},{9,1... | collective-permute-start | bytes 4718600 | tf_op jit(solution)/shard_map/ppermute | solution.py:219
  426.3 5.2 copy-start.20
  428.0 7.0 %copy-start.18 = (bf16[1024,384]{1,0:T(8,128)(2,1)S(1)}, bf16[1024,384]{1,0:T(8,128)(2,1)}, u32[]{:S(2)}) copy-start(bf16[1024,384]{1,0:T(8,128)(2,1)} %copy-done.15) | copy-start | bytes 2359300
  428.0 7.0 %copy-start.19 = (f32[1024,768]{1,0:T(8,128)S(1)}, f32[1024,768]{1,0:T(8,128)}, u32[]{:S(2)}) copy-start(f32[1024,768]{1,0:T(8,128)} %get-tuple-element.129) | copy-start | bytes 9437188
  428.0 3.5 collective-permute-start.11
  434.4 20.4 %collective-permute-start.13 = (bf16[1024,384]{1,0:T(8,128)(2,1)S(1)}, bf16[1024,384]{1,0:T(8,128)(2,1)S(1)}, u32[]{:S(2)}, u32[]{:S(2)}) collective-permute-start(bf16[1024,384]{1,0:T(8,128)(2,1)S(1)} %constant_dynamic-slice_fusion), channel_id=1, source_target_pairs={{0,1},{1,0},{2,3},{3,2},{4,5},{5,4},{6,7},{7,6},{8,9},{9,8},{10,11... | collective-permute-start | bytes 2359304 | tf_op jit(solution)/shard_map/ppermute | solution.py:219
  435.0 19.8 %copy-start.7 = (f32[1024,768]{1,0:T(8,128)S(1)}, f32[1024,768]{1,0:T(8,128)}, u32[]{:S(2)}) copy-start(f32[1024,768]{1,0:T(8,128)} %copy-done.5) | copy-start | bytes 9437188
  436.5 34.5 %copy-start.9 = (f32[1024,768]{1,0:T(8,128)S(1)}, f32[1024,768]{1,0:T(8,128)}, u32[]{:S(2)}) copy-start(f32[1024,768]{1,0:T(8,128)} %copy-done.8) | copy-start | bytes 9437188
  436.6 34.4 %collective-permute-start.16 = (bf16[1024,384]{1,0:T(8,128)(2,1)S(1)}, bf16[1024,384]{1,0:T(8,128)(2,1)S(1)}, u32[]{:S(2)}, u32[]{:S(2)}) collective-permute-start(bf16[1024,384]{1,0:T(8,128)(2,1)S(1)} %dynamic-slice_convert_fusion), channel_id=1, source_target_pairs={{0,1},{1,0},{2,3},{3,2},{4,5},{5,4},{6,7},{7,6},{8,9},{9,8},{10,11... | collective-permute-start | bytes 2359304 | tf_op jit(solution)/shard_map/ppermute | solution.py:219
  573.2 6.5 %copy-start.30 = (bf16[768,384]{1,0:T(8,128)(2,1)S(1)}, bf16[768,384]{1,0:T(8,128)(2,1)}, u32[]{:S(2)}) copy-start(bf16[768,384]{1,0:T(8,128)(2,1)} %get-tuple-element.109) | copy-start | bytes 1769476
  574.7 6.1 %copy-start.29 = (bf16[768,384]{1,0:T(8,128)(2,1)S(1)}, bf16[768,384]{1,0:T(8,128)(2,1)}, u32[]{:S(2)}) copy-start(bf16[768,384]{1,0:T(8,128)(2,1)} %get-tuple-element.110) | copy-start | bytes 1769476
  576.9 5.0 copy-start.28
  584.7 15.3 %collective-permute-start.21 = (bf16[1,2,96,1536]{3,2,1,0:T(8,128)(2,1)S(1)}, bf16[1,2,96,1536]{3,2,1,0:T(8,128)(2,1)S(1)}, u32[]{:S(2)}, u32[]{:S(2)}) collective-permute-start(bf16[1,2,96,1536]{3,2,1,0:T(8,128)(2,1)S(1)} %dynamic-slice_bitcast_fusion.3), channel_id=1, source_target_pairs={{0,4},{4,0},{8,12},{12,8},{16,20},{20,16},{24,28},{28,24},{1,5},{5... | collective-permute-start | bytes 1769480 | tf_op jit(solution)/shard_map/ppermute | solution.py:326
  589.0 13.7 %copy-start.1 = (bf16[768,384]{1,0:T(8,128)(2,1)S(1)}, bf16[768,384]{1,0:T(8,128)(2,1)}, u32[]{:S(2)}) copy-start(bf16[768,384]{1,0:T(8,128)(2,1)} %param.16) | copy-start | bytes 1769476
Sparse Core Ops, SparseCore 0:
  307.3 265.8 all-reduce.2
Sparse Core Ops, SparseCore 1:
  310.1 90.2 reduce-scatter.4
  402.6 49.7 reduce-scatter.8
  454.6 50.9 reduce-scatter.10
  508.6 53.4 reduce-scatter.6
